TPU v7x, 32 devices: a whole 2x2x4 slice. The times are simulated.
32 devices in a mesh: seq: 16 (over z, x, core), head: 2 (over y).
Axes of the slice: x: 2, y: 2, z: 4, core: 2. Of those that a mesh axis runs over, the one named last changes fastest.
Arguments:
- queries: bfloat16 [2048, 8192], P('seq', 'head'), may hold values from -9 to 9
- image_kv: bfloat16 [2, 16384, 1024], P(None, ('seq', 'head')), may hold values from -9 to 9
- image_spans: int32 [16, 2], replicated, may hold values from 0 to 2048, as said below
- image_owner: int32 [16], replicated, may hold values from 0 to 15, as said below
- gate_logit: float32 [1], replicated, may hold values from 0.3 to 1
- grad_out: bfloat16 [2048, 8192], P('seq', 'head'), may hold values from -6 to 6
Outputs:
- attn_output: bfloat16 [2048, 8192], P('seq', 'head')
- grad_queries: bfloat16 [2048, 8192], P('seq', 'head')
- grad_image_kv: bfloat16 [2, 16384, 1024], P(None, ('seq', 'head'))
Inputs may be any that keep to these rules, and one draw needn't show every extreme that they name: `image_owner`: A permutation: every row block of 1024 rows of image_kv holds exactly one image. For each image j, image_spans[j, 0] < image_spans[j, 1], and the span lies within text tokens 128 * image_owner[j] to 128 * (image_owner[j] + 3) - 1; the image held by block 0 is attended up to text token 383.
All inputs are finite; a program needn't handle non-finite values.
Results may differ from a plain program's by a relative error of at most 0.012.
The roundings to bfloat16 on the way count: a program that leaves them out, or rounds other values in their place, can miss the bound.
Values may be sent and summed in bfloat16 or wider, within the bound.
No kernel may reach another device: no remote copies, remote signals or barrier semaphores. Data moves between devices by JAX's collectives and lax.ppermute only.
A program may use at most 192 MiB of HBM per device.

v0:
```python
import functools, math
import jax
import jax.numpy as jnp
from jax import lax
from jax.experimental import pallas as pl
from jax.experimental.pallas import tpu as pltpu
from jax.sharding import PartitionSpec as P

HEADS = 64
KVH = 8
HD = 128
WIN = 3
GROUP = HEADS // KVH
INV_ROOT = 1.0 / math.sqrt(HD)
LOG2E = 1.4426950408889634
NEG = -1e30
BIG = 1e30
VMEM_LIMIT = 36 * 2**20
GRAD_TYPES = (jnp.float32, jnp.bfloat16, jnp.float32)
BLK = 512
UNROLLED = 2
NT = (((1,), (1,)), ((), ()))
NN = (((1,), (0,)), ((), ()))


def dot(a, b, dims=NN):
    return lax.dot_general(a, b, dims, preferred_element_type=jnp.float32)


def cuts_of(sizes):
    starts = [sum(sizes[:p]) for p in range(len(sizes))]
    return [(p, start, start + size) for p, (start, size) in enumerate(zip(starts, sizes))]


def over_blocks(sizes, body):
    for p, start, stop in cuts_of(sizes):
        blk = min(BLK, stop - start)
        if stop - start <= UNROLLED * blk:
            for r in range(0, stop - start, blk):
                body(p, pl.ds(r, blk), pl.ds(start + r, blk))
        else:

            @pl.loop(0, (stop - start) // blk)
            def _(n):
                r = pl.multiple_of(n * blk, blk)
                body(p, pl.ds(r, blk), pl.ds(pl.multiple_of(start + r, blk), blk))


def attend_kernel(sizes, carried, place, *refs):
    head, at = place
    step = pl.program_id(0)
    refs = list(refs)
    spans, gain_ref, q_ref, g_ref = refs[:4]
    del refs[:4]
    kv = [[refs.pop(0) for size in per] for per in sizes]
    del refs[:carried]
    out_ref, dq_ref = refs[:2]
    del refs[:2]
    grads = [refs.pop(0) for d in range(WIN)]
    kt, vt, s, top, total, m_ref, l_ref, o_ref, dqt_ref = refs
    tok = q_ref.shape[0]
    width = GROUP * tok
    gain = gain_ref[0]

    def column(first):
        return pl.ds(pl.multiple_of(first * HD, HD), HD)

    cols = column(at + step)
    slots = column(step)
    text = [column((head + step) * GROUP + g) for g in range(GROUP)]

    q = jnp.concatenate([q_ref[:, cut] for cut in text], axis=0)
    ag = gain * jnp.concatenate([g_ref[:, cut] for cut in text], axis=0).astype(jnp.float32)
    gl = ag.astype(jnp.bfloat16)
    at_tok = lax.rem(lax.broadcasted_iota(jnp.int32, (1, width), 1), tok)
    m_ref[...] = jnp.full_like(m_ref, NEG)
    l_ref[...] = jnp.zeros_like(l_ref)
    o_ref[...] = jnp.zeros_like(o_ref)
    dqt_ref[...] = jnp.zeros_like(dqt_ref)
    active = [spans[2 * d + 1] > spans[2 * d] for d in range(WIN)]
    allowed = [(at_tok >= spans[2 * d]) & (at_tok < spans[2 * d + 1]) for d in range(WIN)]

    for d in range(WIN):

        @pl.when(active[d])
        def _():
            top[...] = jnp.full_like(top, NEG)

            def body(p, rows, image_rows):
                sc = dot(kv[d][p][0, rows, cols], q, NT)
                s[d, image_rows, :] = sc
                top[...] = jnp.maximum(top[...], jnp.max(sc.reshape(-1, 8, width), axis=0))
                kt[d, :, image_rows] = kv[d][p][0, rows, cols].T
                vt[d, :, image_rows] = kv[d][p][1, rows, cols].T

            over_blocks(sizes[d], body)
            highest = jnp.max(top[...], axis=0, keepdims=True)
            m_ref[...] = jnp.maximum(m_ref[...], jnp.where(allowed[d], highest, NEG))

    for d in range(WIN):

        @pl.when(active[d])
        def _():
            shift = jnp.where(allowed[d], m_ref[...] * (INV_ROOT * LOG2E), BIG)
            total[...] = jnp.zeros_like(total)

            def body(p, rows, image_rows):
                e = jnp.exp2(s[d, image_rows, :] * (INV_ROOT * LOG2E) - shift)
                s[d, image_rows, :] = e
                total[...] += jnp.sum(e.reshape(-1, 8, width), axis=0)
                o_ref[...] += dot(vt[d, :, image_rows], e.astype(jnp.bfloat16))

            over_blocks(sizes[d], body)
            l_ref[...] += jnp.sum(total[...], axis=0, keepdims=True)

    l = l_ref[...]
    rl = 1.0 / jnp.where(l > 0, l, 1.0)
    att_t = o_ref[...] * rl
    delta = jnp.sum(ag.T * att_t, axis=0, keepdims=True)
    out = (gain * att_t).T.astype(jnp.bfloat16)
    for g in range(GROUP):
        out_ref[:, g * HD : (g + 1) * HD] = out[g * tok : (g + 1) * tok]

    for d in range(WIN):
        into = grads[d]

        @pl.when(active[d])
        def _():
            def body(p, rows, image_rows):
                dp = dot(kv[d][p][1, rows, cols], gl, NT)
                prob = s[d, image_rows, :] * rl
                ds = (prob * (dp - delta)).astype(jnp.bfloat16)
                into[1, image_rows, slots] = dot(prob.astype(jnp.bfloat16), gl).astype(into.dtype)
                into[0, image_rows, slots] = (dot(ds, q) * INV_ROOT).astype(into.dtype)
                dqt_ref[...] += dot(kt[d, :, image_rows], ds)

            over_blocks(sizes[d], body)

        @pl.when(jnp.logical_not(active[d]))
        def _():
            into[:, :, slots] = jnp.zeros((*into.shape[:2], HD), into.dtype)

    dq = (dqt_ref[...] * INV_ROOT).T.astype(jnp.bfloat16)
    for g in range(GROUP):
        dq_ref[:, g * HD : (g + 1) * HD] = dq[g * tok : (g + 1) * tok]


def attend(spans, gain, queries, grad_out, kv, text, head, at, heads):
    tok = queries.shape[0]
    sizes = [[piece.shape[1] for piece in per] for per in kv]
    img = sum(sizes[0])
    width = GROUP * tok
    flat = [piece for per in kv for piece in per]
    vmem = pl.BlockSpec(memory_space=pltpu.VMEM)
    smem = pl.BlockSpec(memory_space=pltpu.SMEM)
    hbm = pl.BlockSpec(memory_space=pl.ANY)
    text_spec = pl.BlockSpec((tok, GROUP * HD), lambda i: (0, head + i))
    grad_shapes = [
        jax.ShapeDtypeStruct((2, img, heads * HD), GRAD_TYPES[d]) for d in range(WIN)
    ]
    text_shape = jax.ShapeDtypeStruct(queries.shape, jnp.bfloat16)
    n_in = 4 + len(flat)
    carried = tuple(text)
    offset = 0 if text else 2
    results = pl.pallas_call(
        functools.partial(attend_kernel, sizes, len(carried), (head, at)),
        out_shape=[text_shape, text_shape] + grad_shapes,
        grid=(heads,),
        in_specs=[smem, smem, vmem, vmem]
        + [vmem] * len(flat)
        + [hbm] * len(text),
        out_specs=[text_spec] * 2 + [vmem] * len(grad_shapes),
        scratch_shapes=[
            pltpu.VMEM((WIN, HD, img), jnp.bfloat16),
            pltpu.VMEM((WIN, HD, img), jnp.bfloat16),
            pltpu.VMEM((WIN, img, width), jnp.float32),
            pltpu.VMEM((8, width), jnp.float32),
            pltpu.VMEM((8, width), jnp.float32),
            pltpu.VMEM((1, width), jnp.float32),
            pltpu.VMEM((1, width), jnp.float32),
            pltpu.VMEM((HD, width), jnp.float32),
            pltpu.VMEM((HD, width), jnp.float32),
        ],
        input_output_aliases={n_in + i: i + offset for i in range(len(carried))},
        compiler_params=pltpu.CompilerParams(vmem_limit_bytes=VMEM_LIMIT),
        cost_estimate=pl.CostEstimate(
            flops=heads * WIN * img * tok * GROUP * HD, bytes_accessed=heads * 2**20, transcendentals=0
        ),
    )(spans, gain, queries, grad_out, *flat, *carried)
    return tuple(results[:2]), tuple(results[2:])


def shifted(shard, axis, by):
    count = lax.axis_size(axis)
    pairs = [(i, i + by) for i in range(count) if 0 <= i + by < count]
    return lax.ppermute(shard, axis, pairs)


def rotated(shard, axis, by):
    count = lax.axis_size(axis)
    return lax.ppermute(shard, axis, [(i, (i + by) % count) for i in range(count)])


def exchanged(shard, axis):
    return lax.ppermute(shard, axis, [(i, i ^ 1) for i in range(lax.axis_size(axis))])


def after(values, earlier):
    return lax.optimization_barrier((values, earlier))[0]


def slot_bounds(image_spans, image_owner):
    image_count = image_spans.shape[0]
    owner_match = image_owner[None, :] == jnp.arange(image_count, dtype=jnp.int32)[:, None]
    slot_start = jnp.sum(jnp.where(owner_match, image_spans[None, :, 0], 0), axis=1)
    slot_end = jnp.sum(jnp.where(owner_match, image_spans[None, :, 1], 0), axis=1)
    return (slot_start, slot_end)


def shards(queries, image_kv, image_spans, image_owner, gate_logit, grad_out):
    head_count = lax.axis_size("head")
    my_head = lax.axis_index("head")
    my_shard = lax.axis_index("seq")
    odd = my_shard % 2 == 1
    tok_rows = queries.shape[0]
    rows = image_kv.shape[1]
    kv_local = KVH // head_count
    gain = jnp.tanh(gate_logit)
    slot_start, slot_end = slot_bounds(image_spans, image_owner)
    image_ids = jnp.arange(image_spans.shape[0], dtype=jnp.int32)
    bounds = []
    for distance in range(WIN):
        slot_match = image_ids == my_shard - distance
        for slot in (slot_start, slot_end):
            at = jnp.sum(jnp.where(slot_match, slot - my_shard * tok_rows, 0))
            bounds.append(jnp.clip(at, 0, tok_rows))
    spans = jnp.stack(bounds).astype(jnp.int32)

    count = max(kv_local // 2, 1)
    groups = [list(range(count))] + [[head] for head in range(count, kv_local)]
    whole = [rows * head_count]
    pieces = [rows] * head_count

    def columns(source, owner, first):
        start = (owner * kv_local + first) * HD
        return lax.dynamic_slice_in_dim(source, start, count * HD, axis=2)

    arrivals = []
    before = ()
    for first in range(0, kv_local, count):
        source = after(image_kv, before)
        slices = [
            columns(source, (my_head + by) % head_count, first) for by in range(head_count)
        ]
        if not arrivals:
            own = slices[:1]
            own += [rotated(slices[by], "head", by) for by in range(1, head_count)]
            before = spans
            arrivals.append(own)
        else:
            early = slices
            slices = after(slices, arrivals[0][1:])
            own = slices[:1]
            own += [rotated(slices[by], "head", by) for by in range(1, head_count)]
            arrivals.append(own)
    if len(arrivals) == 1:
        early = ()
    far = [
        shifted(after(piece, (spans, early)) if by else piece, "seq", 2)
        for by, piece in enumerate(arrivals[0])
    ]
    near = [jnp.where(odd, f, o) for f, o in zip(far, arrivals[0])]
    near = jnp.concatenate(after(near, arrivals[-1][1:]), axis=1)
    kv = [arrivals[0], [exchanged(near, "seq")], far]
    if len(arrivals) > 1:
        next_own = jnp.concatenate(arrivals[1], axis=1)
        next_far = shifted(next_own, "seq", 2)

    def finish(result, pending, earlier):
        first, keeping, backs = pending
        totals = [None] * len(backs)
        for p in reversed(range(len(backs))):
            back = after(backs[p], earlier)
            totals[p] = (keeping[p] + back.astype(jnp.float32)).astype(jnp.bfloat16)
        if len(backs) < head_count:
            totals = [totals[0][:, start:stop] for p, start, stop in cuts_of(pieces)]
        waited = totals[-1]
        for by in reversed(range(head_count)):
            total = rotated(totals[by], "head", -by) if by else totals[by]
            at = (((my_head + by) % head_count) * kv_local + first) * HD
            result = lax.dynamic_update_slice_in_dim(result, total, at, axis=2)
        return result, waited

    text = ()
    result = jnp.zeros_like(image_kv)
    hold = ()
    pending = []

    for g, group in enumerate(groups):
        last = g + 1 == len(groups)
        split = last
        cuts = pieces if split else whole
        text, grads = attend(
            after(spans, hold),
            gain,
            queries,
            grad_out,
            kv,
            text,
            group[0],
            group[0] % count,
            len(group),
        )
        kept, near_grad, gone = grads
        if len(pending) == 2:
            result, waited = finish(result, pending.pop(0), near_grad)
            near_grad = after(near_grad, waited)
        near_back = exchanged(near_grad, "seq")
        if last and len(pending) > 0:
            result, waited = finish(result, pending.pop(0), near_grad)
            near_back = after(near_back, waited)
        if g == 0 and len(arrivals) > 1:
            next_own, next_far = after((next_own, next_far), near_grad)
            kv = [[next_own], [exchanged(jnp.where(odd, next_far, next_own), "seq")], [next_far]]
        leaving, backs, keeping = [], [], []
        for p, start, stop in reversed(cuts_of(cuts)):
            near_part = near_back[:, start:stop].astype(jnp.float32)
            leaving.append((gone[:, start:stop] + jnp.where(odd, near_part, 0.0)).astype(jnp.bfloat16))
            keeping.append(kept[:, start:stop] + jnp.where(odd, 0.0, near_part))
            backs.append(shifted(leaving[-1], "seq", -2))
        hold = leaving
        pending.append((group[0], keeping[::-1], backs[::-1]))
    for n, item in enumerate(pending):
        result, waited = finish(result, item, leaving if n + 1 < len(pending) else ())
    attn_output, grad_queries = text
    return (attn_output, grad_queries, result)


def solution(mesh):
    placed = (P("seq", "head"), P(None, ("seq", "head"), None), P(), P(), P(), P("seq", "head"))
    return jax.shard_map(
        shards,
        mesh=mesh,
        in_specs=placed,
        out_specs=(P("seq", "head"), P("seq", "head"), P(None, ("seq", "head"), None)),
        check_vma=False,
    )
```

profile of v0, /device:TPU:2, one launch (start us, length us, event | category | flops | bytes accessed | tf_op | source)
XLA Modules:
  0.0 128.9 jit_solution(7400890829045938914)
XLA Ops:
  0.7 1.3 constant_dynamic-slice_fusion.2
  2.0 1.6 %collective-permute-start = (bf16[2,512,256]{2,1,0:T(8,128)(2,1)S(1)}, bf16[2,512,256]{2,1,0:T(8,128)(2,1)S(1)}, u32[]{:S(2)}, u32[]{:S(2)}) collective-permute-start(bf16[2,512,256]{2,1,0:T(8,128)(2,1)S(1)} %get-tuple-element.71), channel_id=1, source_target_pairs={{0,1},{1,0},{2,3},{3,2},{4,5},{5,4},{6,7},{7,6},{8,9},{9,8},{10,11... | collective-permute-start | bytes 1572872 | tf_op jit(solution)/shard_map/ppermute | solution.py:201
  3.6 3.4 %collective-permute-start.1 = (bf16[2,512,256]{2,1,0:T(8,128)(2,1)S(1)}, bf16[2,512,256]{2,1,0:T(8,128)(2,1)S(1)}, u32[]{:S(2)}, u32[]{:S(2)}) collective-permute-start(bf16[2,512,256]{2,1,0:T(8,128)(2,1)S(1)} %get-tuple-element.72.refs_4_), channel_id=1, source_target_pairs={{0,4},{2,6},{4,8},{6,10},{8,12},{10,14},{12,16},{14,18},{16,20},{1... | collective-permute-start | bytes 1572872 | tf_op jit(solution)/shard_map/ppermute | solution.py:196
  7.0 0.1 select_reduce_fusion
  7.2 0.7 fusion.25
  11.8 0.1 stack.27.refs_0_
  11.8 2.1 %constant_dynamic-slice_fusion = (bf16[2,512,256]{2,1,0:T(8,128)(2,1)}, bf16[2,512,256]{2,1,0:T(8,128)(2,1)S(1)}) fusion(bf16[2,512,1024]{2,1,0:T(8,128)(2,1)} %param.7, s32[]{:T(128)S(6)} %select_n.163, s32[]{:T(128)S(6)} %select_n.162), kind=kLoop, calls=%fused_computation.43 | loop fusion | bytes 2097160 | tf_op jit(solution)/shard_map/dynamic_slice | solution.py:246
  13.9 1.8 %collective-permute-done.refs_5_ = bf16[2,512,256]{2,1,0:T(8,128)(2,1)S(1)} collective-permute-done((bf16[2,512,256]{2,1,0:T(8,128)(2,1)S(1)}, bf16[2,512,256]{2,1,0:T(8,128)(2,1)S(1)}, u32[]{:S(2)}, u32[]{:S(2)}) %collective-permute-start) | collective-permute-done | bytes 524320 | tf_op jit(solution)/shard_map/ppermute | solution.py:201
  15.7 3.4 %collective-permute-start.2 = (bf16[2,512,256]{2,1,0:T(8,128)(2,1)S(1)}, bf16[2,512,256]{2,1,0:T(8,128)(2,1)S(1)}, u32[]{:S(2)}, u32[]{:S(2)}) collective-permute-start(bf16[2,512,256]{2,1,0:T(8,128)(2,1)S(1)} %collective-permute-done.refs_5_), channel_id=1, source_target_pairs={{0,4},{2,6},{4,8},{6,10},{8,12},{10,14},{12,16},{14,18},{16,20},{1... | collective-permute-start | bytes 1572872 | tf_op jit(solution)/shard_map/ppermute | solution.py:196
  19.2 1.6 %collective-permute-start.3 = (bf16[2,512,256]{2,1,0:T(8,128)(2,1)}, bf16[2,512,256]{2,1,0:T(8,128)(2,1)S(1)}, u32[]{:S(2)}, u32[]{:S(2)}) collective-permute-start(bf16[2,512,256]{2,1,0:T(8,128)(2,1)} %get-tuple-element.34), channel_id=1, source_target_pairs={{0,1},{1,0},{2,3},{3,2},{4,5},{5,4},{6,7},{7,6},{8,9},{9,8},{10,11... | collective-permute-start | bytes 1572872 | tf_op jit(solution)/shard_map/ppermute | solution.py:201
  20.7 0.0 collective-permute-done.1.refs_7_
  20.7 0.1 broadcast_select_fusion.2
  20.8 9.6 %collective-permute-done.2.refs_8_ = bf16[2,512,256]{2,1,0:T(8,128)(2,1)S(1)} collective-permute-done((bf16[2,512,256]{2,1,0:T(8,128)(2,1)S(1)}, bf16[2,512,256]{2,1,0:T(8,128)(2,1)S(1)}, u32[]{:S(2)}, u32[]{:S(2)}) %collective-permute-start.2) | collective-permute-done | bytes 524320 | tf_op jit(solution)/shard_map/ppermute | solution.py:196
  30.4 0.1 broadcast_select_fusion.1
  30.4 0.0 copy-start
  30.4 0.0 copy-start.1
  30.5 1.5 %collective-permute-done.3 = bf16[2,512,256]{2,1,0:T(8,128)(2,1)S(1)} collective-permute-done((bf16[2,512,256]{2,1,0:T(8,128)(2,1)}, bf16[2,512,256]{2,1,0:T(8,128)(2,1)S(1)}, u32[]{:S(2)}, u32[]{:S(2)}) %collective-permute-start.3) | collective-permute-done | bytes 524320 | tf_op jit(solution)/shard_map/ppermute | solution.py:201
  31.9 0.1 pad_maximum_fusion
  32.0 0.1 collective-permute-start.4
  32.2 3.4 %collective-permute-start.6 = (bf16[2,1024,256]{2,1,0:T(8,128)(2,1)S(1)}, bf16[2,1024,256]{2,1,0:T(8,128)(2,1)S(1)}, u32[]{:S(2)}, u32[]{:S(2)}) collective-permute-start(bf16[2,1024,256]{2,1,0:T(8,128)(2,1)S(1)} %constant_dynamic-update-slice_fusion.refs_4_), channel_id=1, source_target_pairs={{0,4},{2,6},{4,8},{6,10},{8,12},{10,14},{12,16},{14,18},{16,20},{1... | collective-permute-start | bytes 3145736 | tf_op jit(solution)/shard_map/ppermute | solution.py:196
  36.3 0.0 collective-permute-done.4.refs_6_
  36.3 25.2 %shard_map.85 = (bf16[128,4096]{1,0:T(8,128)(2,1)}, bf16[128,4096]{1,0:T(8,128)(2,1)}, f32[2,1024,256]{2,1,0:T(8,128)S(1)}, bf16[2,1024,256]{2,1,0:T(8,128)(2,1)S(1)}, f32[2,1024,256]{2,1,0:T(8,128)S(1)}) custom-call(s32[6]{0:T(128)S(1)} %stack.27.refs_0_, f32[1]{0:T(128)S(6)} %tanh.3.refs_1_, bf16[128,4096]{1,0:T(8,128)(2,1)S(1)} %copy-done, ...), custom_call_target="tpu_custom_call" | custom-call | flops 805306368 | bytes 2097152 | tf_op jit(solution)/shard_map/pallas_call | solution.py:165
  61.5 0.0 collective-permute-done.6.refs_6_
  61.5 0.1 broadcast_select_fusion
  61.6 0.6 collective-permute-start.7
  62.2 2.0 %collective-permute-done.5 = bf16[2,1024,256]{2,1,0:T(8,128)(2,1)S(1)} collective-permute-done((bf16[2,1024,256]{2,1,0:T(8,128)(2,1)S(1)}, bf16[2,1024,256]{2,1,0:T(8,128)(2,1)S(1)}, u32[]{:S(2)}, u32[]{:S(2)}) %collective-permute-start.5) | collective-permute-done | bytes 1048608 | tf_op jit(solution)/shard_map/ppermute | solution.py:205
  64.1 0.3 fusion.1
  64.4 1.9 %collective-permute-start.9 = (bf16[2,1024,256]{2,1,0:T(8,128)(2,1)S(1)}, bf16[2,1024,256]{2,1,0:T(8,128)(2,1)S(1)}, u32[]{:S(2)}, u32[]{:S(2)}) collective-permute-start(bf16[2,1024,256]{2,1,0:T(8,128)(2,1)S(1)} %fusion.1), channel_id=1, source_target_pairs={{4,0},{6,2},{8,4},{10,6},{12,8},{14,10},{16,12},{18,14},{20,16},{2... | collective-permute-start | bytes 3145736 | tf_op jit(solution)/shard_map/ppermute | solution.py:196
  66.4 0.0 collective-permute-done.7.refs_5_
  66.4 13.3 %shard_map.86 = (bf16[128,4096]{1,0:T(8,128)(2,1)}, bf16[128,4096]{1,0:T(8,128)(2,1)}, f32[2,1024,128]{2,1,0:T(8,128)S(1)}, bf16[2,1024,128]{2,1,0:T(8,128)(2,1)S(1)}, f32[2,1024,128]{2,1,0:T(8,128)S(1)}) custom-call(s32[6]{0:T(128)S(1)} %stack.27.refs_0_, f32[1]{0:T(128)S(6)} %tanh.3.refs_1_, ...), custom_call_target="tpu_custom_call", output_to_operand_aliasing={{0}: (7, {}), {1}: (8, {})} | custom-call | flops 402653184 | bytes 1048576 | tf_op jit(solution)/shard_map/pallas_call | solution.py:165
  79.7 0.0 collective-permute-start.8
  79.7 1.9 %collective-permute-done.8 = bf16[2,1024,128]{2,1,0:T(8,128)(2,1)S(1)} collective-permute-done((bf16[2,1024,128]{2,1,0:T(8,128)(2,1)S(1)}, bf16[2,1024,128]{2,1,0:T(8,128)(2,1)S(1)}, u32[]{:S(2)}, u32[]{:S(2)}) %collective-permute-start.8) | collective-permute-done | bytes 524320 | tf_op jit(solution)/shard_map/ppermute | solution.py:205
  81.6 1.0 fusion.6
  82.6 1.9 %collective-permute-start.11 = (bf16[2,1024,128]{2,1,0:T(8,128)(2,1)}, bf16[2,1024,128]{2,1,0:T(8,128)(2,1)}, u32[]{:S(2)}, u32[]{:S(2)}) collective-permute-start(bf16[2,1024,128]{2,1,0:T(8,128)(2,1)} %fusion.6), channel_id=1, source_target_pairs={{4,0},{6,2},{8,4},{10,6},{12,8},{14,10},{16,12},{18,14},{20,16},{2... | collective-permute-start | bytes 1572872 | tf_op jit(solution)/shard_map/ppermute | solution.py:196
  84.6 13.5 %shard_map.87 = (bf16[128,4096]{1,0:T(8,128)(2,1)}, bf16[128,4096]{1,0:T(8,128)(2,1)}, f32[2,1024,128]{2,1,0:T(8,128)S(1)}, bf16[2,1024,128]{2,1,0:T(8,128)(2,1)}, f32[2,1024,128]{2,1,0:T(8,128)S(1)}) custom-call(s32[6]{0:T(128)S(1)} %stack.27.refs_0_, f32[1]{0:T(128)S(6)} %tanh.3.refs_1_, ...), custom_call_target="tpu_custom_call", output_to_operand_aliasing={{0}: (7, {}), {1}: (8, {})} | custom-call | flops 402653184 | bytes 1048576 | tf_op jit(solution)/shard_map/pallas_call | solution.py:165
  98.1 0.0 collective-permute-done.9
  98.1 0.4 fusion.4
  98.5 0.0 copy-start.2
  98.5 1.0 copy-done.2
  99.5 0.9 slice.48
  100.4 1.5 %collective-permute-start.10 = (bf16[2,512,256]{2,1,0:T(8,128)(2,1)}, bf16[2,512,256]{2,1,0:T(8,128)(2,1)S(1)}, u32[]{:S(2)}, u32[]{:S(2)}) collective-permute-start(bf16[2,512,256]{2,1,0:T(8,128)(2,1)} %slice.48), channel_id=1, source_target_pairs={{0,1},{1,0},{2,3},{3,2},{4,5},{5,4},{6,7},{7,6},{8,9},{9,8},{10,11... | collective-permute-start | bytes 1572872 | tf_op jit(solution)/shard_map/ppermute | solution.py:201
  101.9 1.9 %collective-permute-done.11 = bf16[2,1024,128]{2,1,0:T(8,128)(2,1)} collective-permute-done((bf16[2,1024,128]{2,1,0:T(8,128)(2,1)}, bf16[2,1024,128]{2,1,0:T(8,128)(2,1)}, u32[]{:S(2)}, u32[]{:S(2)}) %collective-permute-start.11) | collective-permute-done | bytes 524320 | tf_op jit(solution)/shard_map/ppermute | solution.py:196
  103.8 1.4 %fusion.9 = bf16[2,1024,128]{2,1,0:T(8,128)(2,1)S(1)} fusion(f32[2,1024,128]{2,1,0:T(8,128)S(1)} %get-tuple-element.55, bf16[2,1024,128]{2,1,0:T(8,128)(2,1)} %copy-done.5, bf16[2,1024,128]{2,1,0:T(8,128)(2,1)} %collective-permute-done.11, pred[]{:T(512)S(6)} %eq.55), kind=kLoop, calls=%fused_computation.13 | loop fusion | flops 1572864 | bytes 2621441 | tf_op jit(solution)/shard_map/convert_element_type | solution.py:284
  105.2 1.6 %collective-permute-start.12 = (bf16[2,512,128]{2,1,0:T(8,128)(2,1)S(1)}, bf16[2,512,128]{2,1,0:T(8,128)(2,1)S(1)}, u32[]{:S(2)}, u32[]{:S(2)}) collective-permute-start(bf16[2,512,128]{2,1,0:T(8,128)(2,1)S(1)} %slice.50), channel_id=1, source_target_pairs={{0,1},{1,0},{2,3},{3,2},{4,5},{5,4},{6,7},{7,6},{8,9},{9,8},{10,11... | collective-permute-start | bytes 786440 | tf_op jit(solution)/shard_map/ppermute | solution.py:201
  106.8 1.2 fusion.19
  108.0 0.0 copy-start.3
  108.0 2.1 %collective-permute-start.14 = (bf16[2,512,128]{2,1,0:T(8,128)(2,1)S(1)}, bf16[2,512,128]{2,1,0:T(8,128)(2,1)S(1)}, u32[]{:S(2)}, u32[]{:S(2)}) collective-permute-start(bf16[2,512,128]{2,1,0:T(8,128)(2,1)S(1)} %get-tuple-element.74), channel_id=1, source_target_pairs={{4,0},{6,2},{8,4},{10,6},{12,8},{14,10},{16,12},{18,14},{20,16},{2... | collective-permute-start | bytes 786440 | tf_op jit(solution)/shard_map/ppermute | solution.py:196
  110.0 5.3 %collective-permute-done.10 = bf16[2,512,256]{2,1,0:T(8,128)(2,1)S(1)} collective-permute-done((bf16[2,512,256]{2,1,0:T(8,128)(2,1)}, bf16[2,512,256]{2,1,0:T(8,128)(2,1)S(1)}, u32[]{:S(2)}, u32[]{:S(2)}) %collective-permute-start.10) | collective-permute-done | bytes 524320 | tf_op jit(solution)/shard_map/ppermute | solution.py:201
  115.3 0.3 broadcast_in_dim.64
  115.6 0.1 constant_dynamic-update-slice_fusion.4
  115.6 0.1 slice_dynamic-update-slice_fusion
  115.7 1.9 %collective-permute-start.16 = (bf16[2,512,128]{2,1,0:T(8,128)(2,1)S(1)}, bf16[2,512,128]{2,1,0:T(8,128)(2,1)S(1)}, u32[]{:S(2)}, u32[]{:S(2)}) collective-permute-start(bf16[2,512,128]{2,1,0:T(8,128)(2,1)S(1)} %get-tuple-element.73), channel_id=1, source_target_pairs={{4,0},{6,2},{8,4},{10,6},{12,8},{14,10},{16,12},{18,14},{20,16},{2... | collective-permute-start | bytes 786440 | tf_op jit(solution)/shard_map/ppermute | solution.py:196
  117.6 0.5 collective-permute-done.14
  118.2 1.1 fusion.12
  119.2 1.1 collective-permute-start.15
  120.3 0.2 collective-permute-done.12
  120.5 0.1 constant_dynamic-update-slice_fusion.3
  120.6 0.1 slice_dynamic-update-slice_fusion.1
  120.7 5.3 %collective-permute-done.16 = bf16[2,512,128]{2,1,0:T(8,128)(2,1)S(1)} collective-permute-done((bf16[2,512,128]{2,1,0:T(8,128)(2,1)S(1)}, bf16[2,512,128]{2,1,0:T(8,128)(2,1)S(1)}, u32[]{:S(2)}, u32[]{:S(2)}) %collective-permute-start.16) | collective-permute-done | bytes 262176 | tf_op jit(solution)/shard_map/ppermute | solution.py:196
  126.1 0.3 collective-permute-done.15
  126.3 0.1 constant_dynamic-update-slice_fusion.2
  126.4 1.1 fusion.20
  127.5 0.0 copy-start.4
  127.6 1.3 %copy-done.4 = bf16[2,512,1024]{2,1,0:T(8,128)(2,1)} copy-done((bf16[2,512,1024]{2,1,0:T(8,128)(2,1)}, bf16[2,512,1024]{2,1,0:T(8,128)(2,1)S(1)}, u32[]{:S(2)}) %copy-start.4) | copy-done | bytes 2097176
  (16 shorter events, 0.1 us)
Async XLA Ops:
  0.6 6.4 %copy-start.6 = (s32[16,2]{0,1:T(2,128)S(1)}, s32[16,2]{0,1:T(2,128)}, u32[]{:S(2)}) copy-start(s32[16,2]{0,1:T(2,128)} %param.8) | copy-start | bytes 388
  0.6 6.4 %copy-start.7 = (s32[16]{0:T(128)S(1)}, s32[16]{0:T(128)}, u32[]{:S(2)}) copy-start(s32[16]{0:T(128)} %param.9) | copy-start | bytes 196
  2.0 13.7 %collective-permute-start = (bf16[2,512,256]{2,1,0:T(8,128)(2,1)S(1)}, bf16[2,512,256]{2,1,0:T(8,128)(2,1)S(1)}, u32[]{:S(2)}, u32[]{:S(2)}) collective-permute-start(bf16[2,512,256]{2,1,0:T(8,128)(2,1)S(1)} %get-tuple-element.71), channel_id=1, source_target_pairs={{0,1},{1,0},{2,3},{3,2},{4,5},{5,4},{6,7},{7,6},{8,9},{9,8},{10,11... | collective-permute-start | bytes 1572872 | tf_op jit(solution)/shard_map/ppermute | solution.py:201
  3.6 17.2 %collective-permute-start.1 = (bf16[2,512,256]{2,1,0:T(8,128)(2,1)S(1)}, bf16[2,512,256]{2,1,0:T(8,128)(2,1)S(1)}, u32[]{:S(2)}, u32[]{:S(2)}) collective-permute-start(bf16[2,512,256]{2,1,0:T(8,128)(2,1)S(1)} %get-tuple-element.72.refs_4_), channel_id=1, source_target_pairs={{0,4},{2,6},{4,8},{6,10},{8,12},{10,14},{12,16},{14,18},{16,20},{1... | collective-permute-start | bytes 1572872 | tf_op jit(solution)/shard_map/ppermute | solution.py:196
  15.7 14.7 %collective-permute-start.2 = (bf16[2,512,256]{2,1,0:T(8,128)(2,1)S(1)}, bf16[2,512,256]{2,1,0:T(8,128)(2,1)S(1)}, u32[]{:S(2)}, u32[]{:S(2)}) collective-permute-start(bf16[2,512,256]{2,1,0:T(8,128)(2,1)S(1)} %collective-permute-done.refs_5_), channel_id=1, source_target_pairs={{0,4},{2,6},{4,8},{6,10},{8,12},{10,14},{12,16},{14,18},{16,20},{1... | collective-permute-start | bytes 1572872 | tf_op jit(solution)/shard_map/ppermute | solution.py:196
  19.2 12.8 %collective-permute-start.3 = (bf16[2,512,256]{2,1,0:T(8,128)(2,1)}, bf16[2,512,256]{2,1,0:T(8,128)(2,1)S(1)}, u32[]{:S(2)}, u32[]{:S(2)}) collective-permute-start(bf16[2,512,256]{2,1,0:T(8,128)(2,1)} %get-tuple-element.34), channel_id=1, source_target_pairs={{0,1},{1,0},{2,3},{3,2},{4,5},{5,4},{6,7},{7,6},{8,9},{9,8},{10,11... | collective-permute-start | bytes 1572872 | tf_op jit(solution)/shard_map/ppermute | solution.py:201
  30.4 5.9 %copy-start = (bf16[128,4096]{1,0:T(8,128)(2,1)S(1)}, bf16[128,4096]{1,0:T(8,128)(2,1)}, u32[]{:S(2)}) copy-start(bf16[128,4096]{1,0:T(8,128)(2,1)} %refs_2_.5) | copy-start | bytes 3145732
  30.4 5.9 %copy-start.1 = (bf16[128,4096]{1,0:T(8,128)(2,1)S(1)}, bf16[128,4096]{1,0:T(8,128)(2,1)}, u32[]{:S(2)}) copy-start(bf16[128,4096]{1,0:T(8,128)(2,1)} %refs_3_.5) | copy-start | bytes 3145732
  32.0 4.3 %collective-permute-start.4 = (bf16[2,1024,256]{2,1,0:T(8,128)(2,1)S(1)}, bf16[2,1024,256]{2,1,0:T(8,128)(2,1)S(1)}, u32[]{:S(2)}, u32[]{:S(2)}) collective-permute-start(bf16[2,1024,256]{2,1,0:T(8,128)(2,1)S(1)} %pad_maximum_fusion), channel_id=1, source_target_pairs={{0,2},{2,0},{4,6},{6,4},{8,10},{10,8},{12,14},{14,12},{16,18},{18,... | collective-permute-start | bytes 3145736 | tf_op jit(solution)/shard_map/ppermute | solution.py:205
  32.2 29.3 %collective-permute-start.6 = (bf16[2,1024,256]{2,1,0:T(8,128)(2,1)S(1)}, bf16[2,1024,256]{2,1,0:T(8,128)(2,1)S(1)}, u32[]{:S(2)}, u32[]{:S(2)}) collective-permute-start(bf16[2,1024,256]{2,1,0:T(8,128)(2,1)S(1)} %constant_dynamic-update-slice_fusion.refs_4_), channel_id=1, source_target_pairs={{0,4},{2,6},{4,8},{6,10},{8,12},{10,14},{12,16},{14,18},{16,20},{1... | collective-permute-start | bytes 3145736 | tf_op jit(solution)/shard_map/ppermute | solution.py:196
  61.5 2.7 %collective-permute-start.5 = (bf16[2,1024,256]{2,1,0:T(8,128)(2,1)S(1)}, bf16[2,1024,256]{2,1,0:T(8,128)(2,1)S(1)}, u32[]{:S(2)}, u32[]{:S(2)}) collective-permute-start(bf16[2,1024,256]{2,1,0:T(8,128)(2,1)S(1)} %get-tuple-element.38), channel_id=1, source_target_pairs={{0,2},{2,0},{4,6},{6,4},{8,10},{10,8},{12,14},{14,12},{16,18},{18,... | collective-permute-start | bytes 3145736 | tf_op jit(solution)/shard_map/ppermute | solution.py:205
  61.6 4.8 %collective-permute-start.7 = (bf16[2,1024,256]{2,1,0:T(8,128)(2,1)S(1)}, bf16[2,1024,256]{2,1,0:T(8,128)(2,1)S(1)}, u32[]{:S(2)}, u32[]{:S(2)}) collective-permute-start(bf16[2,1024,256]{2,1,0:T(8,128)(2,1)S(1)} %broadcast_select_fusion), channel_id=1, source_target_pairs={{0,2},{2,0},{4,6},{6,4},{8,10},{10,8},{12,14},{14,12},{16,18},{18,... | collective-permute-start | bytes 3145736 | tf_op jit(solution)/shard_map/ppermute | solution.py:205
  64.4 33.6 %collective-permute-start.9 = (bf16[2,1024,256]{2,1,0:T(8,128)(2,1)S(1)}, bf16[2,1024,256]{2,1,0:T(8,128)(2,1)S(1)}, u32[]{:S(2)}, u32[]{:S(2)}) collective-permute-start(bf16[2,1024,256]{2,1,0:T(8,128)(2,1)S(1)} %fusion.1), channel_id=1, source_target_pairs={{4,0},{6,2},{8,4},{10,6},{12,8},{14,10},{16,12},{18,14},{20,16},{2... | collective-permute-start | bytes 3145736 | tf_op jit(solution)/shard_map/ppermute | solution.py:196
  79.7 1.9 %collective-permute-start.8 = (bf16[2,1024,128]{2,1,0:T(8,128)(2,1)S(1)}, bf16[2,1024,128]{2,1,0:T(8,128)(2,1)S(1)}, u32[]{:S(2)}, u32[]{:S(2)}) collective-permute-start(bf16[2,1024,128]{2,1,0:T(8,128)(2,1)S(1)} %get-tuple-element.46), channel_id=1, source_target_pairs={{0,2},{2,0},{4,6},{6,4},{8,10},{10,8},{12,14},{14,12},{16,18},{18,... | collective-permute-start | bytes 1572872 | tf_op jit(solution)/shard_map/ppermute | solution.py:205
  81.6 16.5 %copy-start.5 = (bf16[2,1024,128]{2,1,0:T(8,128)(2,1)}, bf16[2,1024,128]{2,1,0:T(8,128)(2,1)S(1)}, u32[]{:S(2)}) copy-start(bf16[2,1024,128]{2,1,0:T(8,128)(2,1)S(1)} %collective-permute-done.8) | copy-start | bytes 1572868
  82.6 21.1 %collective-permute-start.11 = (bf16[2,1024,128]{2,1,0:T(8,128)(2,1)}, bf16[2,1024,128]{2,1,0:T(8,128)(2,1)}, u32[]{:S(2)}, u32[]{:S(2)}) collective-permute-start(bf16[2,1024,128]{2,1,0:T(8,128)(2,1)} %fusion.6), channel_id=1, source_target_pairs={{4,0},{6,2},{8,4},{10,6},{12,8},{14,10},{16,12},{18,14},{20,16},{2... | collective-permute-start | bytes 1572872 | tf_op jit(solution)/shard_map/ppermute | solution.py:196
  98.5 1.0 copy-start.2
  100.4 6.4 %collective-permute-start.13 = (bf16[2,1024,128]{2,1,0:T(8,128)(2,1)}, bf16[2,1024,128]{2,1,0:T(8,128)(2,1)}, u32[]{:S(2)}, u32[]{:S(2)}) collective-permute-start(bf16[2,1024,128]{2,1,0:T(8,128)(2,1)} %get-tuple-element.56), channel_id=1, source_target_pairs={{0,2},{2,0},{4,6},{6,4},{8,10},{10,8},{12,14},{14,12},{16,18},{18,... | collective-permute-start | bytes 1572872 | tf_op jit(solution)/shard_map/ppermute | solution.py:205
  100.4 14.9 %collective-permute-start.10 = (bf16[2,512,256]{2,1,0:T(8,128)(2,1)}, bf16[2,512,256]{2,1,0:T(8,128)(2,1)S(1)}, u32[]{:S(2)}, u32[]{:S(2)}) collective-permute-start(bf16[2,512,256]{2,1,0:T(8,128)(2,1)} %slice.48), channel_id=1, source_target_pairs={{0,1},{1,0},{2,3},{3,2},{4,5},{5,4},{6,7},{7,6},{8,9},{9,8},{10,11... | collective-permute-start | bytes 1572872 | tf_op jit(solution)/shard_map/ppermute | solution.py:201
  105.2 15.3 %collective-permute-start.12 = (bf16[2,512,128]{2,1,0:T(8,128)(2,1)S(1)}, bf16[2,512,128]{2,1,0:T(8,128)(2,1)S(1)}, u32[]{:S(2)}, u32[]{:S(2)}) collective-permute-start(bf16[2,512,128]{2,1,0:T(8,128)(2,1)S(1)} %slice.50), channel_id=1, source_target_pairs={{0,1},{1,0},{2,3},{3,2},{4,5},{5,4},{6,7},{7,6},{8,9},{9,8},{10,11... | collective-permute-start | bytes 786440 | tf_op jit(solution)/shard_map/ppermute | solution.py:201
  108.0 7.7 %copy-start.3 = (bf16[2,1024,256]{2,1,0:T(8,128)(2,1)S(1)}, bf16[2,1024,256]{2,1,0:T(8,128)(2,1)}, u32[]{:S(2)}) copy-start(bf16[2,1024,256]{2,1,0:T(8,128)(2,1)} %copy-done.2) | copy-start | bytes 3145732
  108.0 10.2 %collective-permute-start.14 = (bf16[2,512,128]{2,1,0:T(8,128)(2,1)S(1)}, bf16[2,512,128]{2,1,0:T(8,128)(2,1)S(1)}, u32[]{:S(2)}, u32[]{:S(2)}) collective-permute-start(bf16[2,512,128]{2,1,0:T(8,128)(2,1)S(1)} %get-tuple-element.74), channel_id=1, source_target_pairs={{4,0},{6,2},{8,4},{10,6},{12,8},{14,10},{16,12},{18,14},{20,16},{2... | collective-permute-start | bytes 786440 | tf_op jit(solution)/shard_map/ppermute | solution.py:196
  115.7 10.3 %collective-permute-start.16 = (bf16[2,512,128]{2,1,0:T(8,128)(2,1)S(1)}, bf16[2,512,128]{2,1,0:T(8,128)(2,1)S(1)}, u32[]{:S(2)}, u32[]{:S(2)}) collective-permute-start(bf16[2,512,128]{2,1,0:T(8,128)(2,1)S(1)} %get-tuple-element.73), channel_id=1, source_target_pairs={{4,0},{6,2},{8,4},{10,6},{12,8},{14,10},{16,12},{18,14},{20,16},{2... | collective-permute-start | bytes 786440 | tf_op jit(solution)/shard_map/ppermute | solution.py:196
  119.2 7.1 %collective-permute-start.15 = (bf16[2,512,128]{2,1,0:T(8,128)(2,1)S(1)}, bf16[2,512,128]{2,1,0:T(8,128)(2,1)S(1)}, u32[]{:S(2)}, u32[]{:S(2)}) collective-permute-start(bf16[2,512,128]{2,1,0:T(8,128)(2,1)S(1)} %fusion.12), channel_id=1, source_target_pairs={{0,1},{1,0},{2,3},{3,2},{4,5},{5,4},{6,7},{7,6},{8,9},{9,8},{10,11... | collective-permute-start | bytes 786440 | tf_op jit(solution)/shard_map/ppermute | solution.py:201
  127.5 1.3 %copy-start.4 = (bf16[2,512,1024]{2,1,0:T(8,128)(2,1)}, bf16[2,512,1024]{2,1,0:T(8,128)(2,1)S(1)}, u32[]{:S(2)}) copy-start(bf16[2,512,1024]{2,1,0:T(8,128)(2,1)S(1)} %fusion.20) | copy-start | bytes 6291460
where the time goes:
time: 131 us; the launch traced here: 129 us
  Pallas kernels  52 us (40%)
  waiting for transfers between devices  30.2 us (23%)
  starting transfers between devices  26.1 us (20%)
  other arithmetic  7.61 us (6%)
  local copies, waits for them, and re-layouts  7.35 us (6%)
  between operations  5.54 us (4%)
    pallas_call x3, Pallas kernels, attend(): pl.pallas_call(functools.partial(attend_kernel, sizes, len(carried), (hea...  52 us
    ppermute x7, starting transfers between devices, shifted(): return lax.ppermute(shard, axis, pairs)  18.1 us
    ppermute x7, waiting for transfers between devices, shifted(): return lax.ppermute(shard, axis, pairs)  17.3 us
    ppermute x5, waiting for transfers between devices, rotated(): lax.ppermute(shard, axis, [(i, (i + by) % count) for i in range(count)])  9.04 us
    ppermute x5, starting transfers between devices, rotated(): lax.ppermute(shard, axis, [(i, (i + by) % count) for i in range(count)])  7.34 us
    ppermute x5, waiting for transfers between devices, exchanged(): lax.ppermute(shard, axis, [(i, i ^ 1) for i in range(lax.axis_size(axis))])  3.88 us
    dynamic_slice x2, local copies, waits for them, and re-layouts, columns(): return lax.dynamic_slice_in_dim(source, start, count * HD, axis=2)  3.35 us
    convert_element_type x3, other arithmetic, finish(): totals[p] = (keeping[p] + back.astype(jnp.float32)).astype(jnp.bfloat16)  2.88 us
  transfers between devices with their start and end apart: 17, of which 11 were waited for; matrix products, arithmetic and copies ran while one was open for 8% of the time, Pallas kernels for 40%

commit v1 on v0

--- a/solution.py
+++ b/solution.py
@@ -183,9 +183,7 @@
         ],
         input_output_aliases={n_in + i: i + offset for i in range(len(carried))},
         compiler_params=pltpu.CompilerParams(vmem_limit_bytes=VMEM_LIMIT),
-        cost_estimate=pl.CostEstimate(
-            flops=heads * WIN * img * tok * GROUP * HD, bytes_accessed=heads * 2**20, transcendentals=0
-        ),
+        cost_estimate=pl.CostEstimate(flops=1, bytes_accessed=1, transcendentals=0),
     )(spans, gain, queries, grad_out, *flat, *carried)
     return tuple(results[:2]), tuple(results[2:])
 
@@ -250,8 +248,11 @@
     for first in range(0, kv_local, count):
         source = after(image_kv, before)
         slices = [
-            columns(source, (my_head + by) % head_count, first) for by in range(head_count)
+            columns(source, (my_head + by) % head_count, first) for by in range(1, head_count)
         ]
+        if not arrivals:
+            source = after(image_kv, slices)
+        slices = [columns(source, my_head, first)] + slices
         if not arrivals:
             own = slices[:1]
             own += [rotated(slices[by], "head", by) for by in range(1, head_count)]
@@ -276,23 +277,23 @@
         next_own = jnp.concatenate(arrivals[1], axis=1)
         next_far = shifted(next_own, "seq", 2)
 
-    def finish(result, pending, earlier):
+    def finish(pending, earlier):
         first, keeping, backs = pending
-        totals = [None] * len(backs)
-        for p in reversed(range(len(backs))):
-            back = after(backs[p], earlier)
-            totals[p] = (keeping[p] + back.astype(jnp.float32)).astype(jnp.bfloat16)
+        backs = [after(back, earlier) for back in backs]
+        totals = [
+            (keep + back.astype(jnp.float32)).astype(jnp.bfloat16)
+            for keep, back in zip(keeping, backs)
+        ]
         if len(backs) < head_count:
             totals = [totals[0][:, start:stop] for p, start, stop in cuts_of(pieces)]
-        waited = totals[-1]
+        placed = []
         for by in reversed(range(head_count)):
             total = rotated(totals[by], "head", -by) if by else totals[by]
-            at = (((my_head + by) % head_count) * kv_local + first) * HD
-            result = lax.dynamic_update_slice_in_dim(result, total, at, axis=2)
-        return result, waited
+            placed.append((total, (((my_head + by) % head_count) * kv_local + first) * HD))
+        return placed, totals
 
     text = ()
-    result = jnp.zeros_like(image_kv)
+    placed = []
     hold = ()
     pending = []
 
@@ -313,11 +314,13 @@
         )
         kept, near_grad, gone = grads
         if len(pending) == 2:
-            result, waited = finish(result, pending.pop(0), near_grad)
+            more, waited = finish(pending.pop(0), near_grad)
+            placed += more
             near_grad = after(near_grad, waited)
         near_back = exchanged(near_grad, "seq")
         if last and len(pending) > 0:
-            result, waited = finish(result, pending.pop(0), near_grad)
+            more, waited = finish(pending.pop(0), near_grad)
+            placed += more
             near_back = after(near_back, waited)
         if g == 0 and len(arrivals) > 1:
             next_own, next_far = after((next_own, next_far), near_grad)
@@ -330,8 +333,12 @@
             backs.append(shifted(leaving[-1], "seq", -2))
         hold = leaving
         pending.append((group[0], keeping[::-1], backs[::-1]))
-    for n, item in enumerate(pending):
-        result, waited = finish(result, item, leaving if n + 1 < len(pending) else ())
+    more, waited = finish(pending.pop(), ())
+    for item in pending:
+        placed += finish(item, leaving)[0]
+    result = jnp.zeros_like(image_kv)
+    for columns_of, at in [(after(total, waited[-1]), at) for total, at in placed] + more:
+        result = lax.dynamic_update_slice_in_dim(result, columns_of, at, axis=2)
     attn_output, grad_queries = text
     return (attn_output, grad_queries, result)
 

time: 131 us -> 127 us (0.969)
  other arithmetic: 7.61 us -> 4.62 us
    ppermute x7, waiting for transfers between devices: 17.3 us -> 21.8 us  [shifted(): return lax.ppermute(shard, axis, pairs)]
    ppermute x5, waiting for transfers between devices: 9.04 us -> 4.83 us  [rotated(): lax.ppermute(shard, axis, [(i, (i + by) % count) for i in range(count)])]
    convert_element_type x3, other arithmetic: 2.47 us -> 0.53 us  [shards(): (gone[:, start:stop] + jnp.where(odd, near_part, 0.0)).astype(jnp.bfloat16)]
    dynamic_slice x2 -> x3, local copies, waits for them, and re-layouts: 3.35 us -> 4.23 us  [columns(): return lax.dynamic_slice_in_dim(source, start, count * HD, axis=2)]
  transfers between devices with their start and end apart: 17 -> 17, of which waited for: 11 -> 9; matrix products, arithmetic and copies ran while one was open for 8% -> 8% of each run, Pallas kernels for 40% -> 41%
where the time goes in v1:
time: 127 us; the launch traced here: 126 us
  Pallas kernels  51.7 us (41%)
  waiting for transfers between devices  30.5 us (24%)
  starting transfers between devices  25.7 us (20%)
  local copies, waits for them, and re-layouts  7.96 us (6%)
  between operations  5.59 us (4%)
  other arithmetic  4.62 us (4%)
    pallas_call x3, Pallas kernels, attend(): pl.pallas_call(functools.partial(attend_kernel, sizes, len(carried), (hea...  51.7 us
    ppermute x7, waiting for transfers between devices, shifted(): return lax.ppermute(shard, axis, pairs)  21.8 us
    ppermute x7, starting transfers between devices, shifted(): return lax.ppermute(shard, axis, pairs)  18.4 us
    ppermute x5, starting transfers between devices, rotated(): lax.ppermute(shard, axis, [(i, (i + by) % count) for i in range(count)])  6.67 us
    ppermute x5, waiting for transfers between devices, rotated(): lax.ppermute(shard, axis, [(i, (i + by) % count) for i in range(count)])  4.83 us
    dynamic_slice x3, local copies, waits for them, and re-layouts, columns(): return lax.dynamic_slice_in_dim(source, start, count * HD, axis=2)  4.23 us
    ppermute x5, waiting for transfers between devices, exchanged(): lax.ppermute(shard, axis, [(i, i ^ 1) for i in range(lax.axis_size(axis))])  3.88 us
  transfers between devices with their start and end apart: 17, of which 9 were waited for; matrix products, arithmetic and copies ran while one was open for 8% of the time, Pallas kernels for 41%

profile of v1, /device:TPU:2, one launch (start us, length us, event | category | flops | bytes accessed | tf_op | source)
XLA Modules:
  0.0 126.1 jit_solution(1842409407750141590)
XLA Ops:
  0.7 1.1 constant_dynamic-slice_fusion.3
  1.8 1.6 %collective-permute-start = (bf16[2,512,256]{2,1,0:T(8,128)(2,1)S(1)}, bf16[2,512,256]{2,1,0:T(8,128)(2,1)S(1)}, u32[]{:S(2)}, u32[]{:S(2)}) collective-permute-start(bf16[2,512,256]{2,1,0:T(8,128)(2,1)S(1)} %constant_dynamic-slice_fusion.3), channel_id=1, source_target_pairs={{0,1},{1,0},{2,3},{3,2},{4,5},{5,4},{6,7},{7,6},{8,9},{9,8},{10,11... | collective-permute-start | bytes 1572872 | tf_op jit(solution)/shard_map/ppermute | solution.py:199
  3.3 1.1 constant_dynamic-slice_fusion.2.refs_4_
  4.4 3.5 %collective-permute-start.1 = (bf16[2,512,256]{2,1,0:T(8,128)(2,1)S(1)}, bf16[2,512,256]{2,1,0:T(8,128)(2,1)S(1)}, u32[]{:S(2)}, u32[]{:S(2)}) collective-permute-start(bf16[2,512,256]{2,1,0:T(8,128)(2,1)S(1)} %constant_dynamic-slice_fusion.2.refs_4_), channel_id=1, source_target_pairs={{0,4},{2,6},{4,8},{6,10},{8,12},{10,14},{12,16},{14,18},{16,20},{1... | collective-permute-start | bytes 1572872 | tf_op jit(solution)/shard_map/ppermute | solution.py:194
  7.9 0.1 select_reduce_fusion
  8.0 0.8 fusion.25
  12.7 0.1 stack.27.refs_0_
  12.8 2.1 %constant_dynamic-slice_fusion = (bf16[2,512,256]{2,1,0:T(8,128)(2,1)}, bf16[2,512,256]{2,1,0:T(8,128)(2,1)S(1)}) fusion(bf16[2,512,1024]{2,1,0:T(8,128)(2,1)} %param.7, s32[]{:T(128)S(6)} %select_n.162, s32[]{:T(128)S(6)} %select_n.161), kind=kLoop, calls=%fused_computation.43 | loop fusion | bytes 2097160 | tf_op jit(solution)/shard_map/dynamic_slice | solution.py:244
  14.9 0.6 collective-permute-done.refs_5_
  15.5 3.4 %collective-permute-start.2 = (bf16[2,512,256]{2,1,0:T(8,128)(2,1)S(1)}, bf16[2,512,256]{2,1,0:T(8,128)(2,1)S(1)}, u32[]{:S(2)}, u32[]{:S(2)}) collective-permute-start(bf16[2,512,256]{2,1,0:T(8,128)(2,1)S(1)} %collective-permute-done.refs_5_), channel_id=1, source_target_pairs={{0,4},{2,6},{4,8},{6,10},{8,12},{10,14},{12,16},{14,18},{16,20},{1... | collective-permute-start | bytes 1572872 | tf_op jit(solution)/shard_map/ppermute | solution.py:194
  18.9 1.6 %collective-permute-start.3 = (bf16[2,512,256]{2,1,0:T(8,128)(2,1)}, bf16[2,512,256]{2,1,0:T(8,128)(2,1)S(1)}, u32[]{:S(2)}, u32[]{:S(2)}) collective-permute-start(bf16[2,512,256]{2,1,0:T(8,128)(2,1)} %get-tuple-element.40), channel_id=1, source_target_pairs={{0,1},{1,0},{2,3},{3,2},{4,5},{5,4},{6,7},{7,6},{8,9},{9,8},{10,11... | collective-permute-start | bytes 1572872 | tf_op jit(solution)/shard_map/ppermute | solution.py:199
  20.5 0.0 collective-permute-done.1.refs_7_
  20.5 1.2 broadcast_select_fusion.2
  21.7 9.2 %collective-permute-done.2.refs_8_ = bf16[2,512,256]{2,1,0:T(8,128)(2,1)S(1)} collective-permute-done((bf16[2,512,256]{2,1,0:T(8,128)(2,1)S(1)}, bf16[2,512,256]{2,1,0:T(8,128)(2,1)S(1)}, u32[]{:S(2)}, u32[]{:S(2)}) %collective-permute-start.2) | collective-permute-done | bytes 524320 | tf_op jit(solution)/shard_map/ppermute | solution.py:194
  30.9 0.1 broadcast_select_fusion.1
  31.0 0.0 copy-start
  31.0 0.0 copy-start.1
  31.0 0.7 collective-permute-done.3
  31.7 0.1 pad_maximum_fusion
  31.8 0.1 collective-permute-start.4
  32.0 3.8 %collective-permute-start.6 = (bf16[2,1024,256]{2,1,0:T(8,128)(2,1)S(1)}, bf16[2,1024,256]{2,1,0:T(8,128)(2,1)S(1)}, u32[]{:S(2)}, u32[]{:S(2)}) collective-permute-start(bf16[2,1024,256]{2,1,0:T(8,128)(2,1)S(1)} %constant_dynamic-update-slice_fusion.refs_4_), channel_id=1, source_target_pairs={{0,4},{2,6},{4,8},{6,10},{8,12},{10,14},{12,16},{14,18},{16,20},{1... | collective-permute-start | bytes 3145736 | tf_op jit(solution)/shard_map/ppermute | solution.py:194
  36.5 0.0 collective-permute-done.4.refs_6_
  36.5 25.1 %shard_map.85 = (bf16[128,4096]{1,0:T(8,128)(2,1)}, bf16[128,4096]{1,0:T(8,128)(2,1)}, f32[2,1024,256]{2,1,0:T(8,128)S(1)}, bf16[2,1024,256]{2,1,0:T(8,128)(2,1)S(1)}, f32[2,1024,256]{2,1,0:T(8,128)S(1)}) custom-call(s32[6]{0:T(128)S(1)} %stack.27.refs_0_, f32[1]{0:T(128)S(6)} %tanh.3.refs_1_, bf16[128,4096]{1,0:T(8,128)(2,1)S(1)} %copy-done, ...), custom_call_target="tpu_custom_call" | custom-call | flops 1 | bytes 1 | tf_op jit(solution)/shard_map/pallas_call | solution.py:165
  61.6 0.0 collective-permute-start.5
  61.6 0.0 collective-permute-done.6.refs_6_
  61.6 0.1 broadcast_select_fusion
  61.7 0.6 collective-permute-start.7
  62.3 2.0 %collective-permute-done.5 = bf16[2,1024,256]{2,1,0:T(8,128)(2,1)S(1)} collective-permute-done((bf16[2,1024,256]{2,1,0:T(8,128)(2,1)S(1)}, bf16[2,1024,256]{2,1,0:T(8,128)(2,1)S(1)}, u32[]{:S(2)}, u32[]{:S(2)}) %collective-permute-start.5) | collective-permute-done | bytes 1048608 | tf_op jit(solution)/shard_map/ppermute | solution.py:203
  64.3 0.2 fusion.1
  64.5 1.9 %collective-permute-start.9 = (bf16[2,1024,256]{2,1,0:T(8,128)(2,1)S(1)}, bf16[2,1024,256]{2,1,0:T(8,128)(2,1)S(1)}, u32[]{:S(2)}, u32[]{:S(2)}) collective-permute-start(bf16[2,1024,256]{2,1,0:T(8,128)(2,1)S(1)} %fusion.1), channel_id=1, source_target_pairs={{4,0},{6,2},{8,4},{10,6},{12,8},{14,10},{16,12},{18,14},{20,16},{2... | collective-permute-start | bytes 3145736 | tf_op jit(solution)/shard_map/ppermute | solution.py:194
  66.4 0.0 collective-permute-done.7.refs_5_
  66.5 13.2 %shard_map.86 = (bf16[128,4096]{1,0:T(8,128)(2,1)}, bf16[128,4096]{1,0:T(8,128)(2,1)}, f32[2,1024,128]{2,1,0:T(8,128)S(1)}, bf16[2,1024,128]{2,1,0:T(8,128)(2,1)S(1)}, f32[2,1024,128]{2,1,0:T(8,128)S(1)}) custom-call(s32[6]{0:T(128)S(1)} %stack.27.refs_0_, f32[1]{0:T(128)S(6)} %tanh.3.refs_1_, ...), custom_call_target="tpu_custom_call", output_to_operand_aliasing={{0}: (7, {}), {1}: (8, {})} | custom-call | flops 1 | bytes 1 | tf_op jit(solution)/shard_map/pallas_call | solution.py:165
  79.7 0.0 collective-permute-start.8
  79.7 1.9 %collective-permute-done.8 = bf16[2,1024,128]{2,1,0:T(8,128)(2,1)S(1)} collective-permute-done((bf16[2,1024,128]{2,1,0:T(8,128)(2,1)S(1)}, bf16[2,1024,128]{2,1,0:T(8,128)(2,1)S(1)}, u32[]{:S(2)}, u32[]{:S(2)}) %collective-permute-start.8) | collective-permute-done | bytes 524320 | tf_op jit(solution)/shard_map/ppermute | solution.py:203
  81.6 0.1 fusion.6
  81.8 1.9 %collective-permute-start.12 = (bf16[2,1024,128]{2,1,0:T(8,128)(2,1)S(1)}, bf16[2,1024,128]{2,1,0:T(8,128)(2,1)S(1)}, u32[]{:S(2)}, u32[]{:S(2)}) collective-permute-start(bf16[2,1024,128]{2,1,0:T(8,128)(2,1)S(1)} %fusion.6), channel_id=1, source_target_pairs={{4,0},{6,2},{8,4},{10,6},{12,8},{14,10},{16,12},{18,14},{20,16},{2... | collective-permute-start | bytes 1572872 | tf_op jit(solution)/shard_map/ppermute | solution.py:194
  83.7 13.3 %shard_map.87 = (bf16[128,4096]{1,0:T(8,128)(2,1)}, bf16[128,4096]{1,0:T(8,128)(2,1)}, f32[2,1024,128]{2,1,0:T(8,128)S(1)}, bf16[2,1024,128]{2,1,0:T(8,128)(2,1)S(1)}, f32[2,1024,128]{2,1,0:T(8,128)S(1)}) custom-call(s32[6]{0:T(128)S(1)} %stack.27.refs_0_, f32[1]{0:T(128)S(6)} %tanh.3.refs_1_, ...), custom_call_target="tpu_custom_call", output_to_operand_aliasing={{0}: (7, {}), {1}: (8, {})} | custom-call | flops 1 | bytes 1 | tf_op jit(solution)/shard_map/pallas_call | solution.py:165
  97.0 0.0 collective-permute-done.9
  97.0 0.4 fusion.4
  97.4 0.9 fusion.27
  98.2 1.1 collective-permute-start.10
  99.3 0.0 collective-permute-start.11
  99.4 4.4 %collective-permute-done.12 = bf16[2,1024,128]{2,1,0:T(8,128)(2,1)S(1)} collective-permute-done((bf16[2,1024,128]{2,1,0:T(8,128)(2,1)S(1)}, bf16[2,1024,128]{2,1,0:T(8,128)(2,1)S(1)}, u32[]{:S(2)}, u32[]{:S(2)}) %collective-permute-start.12) | collective-permute-done | bytes 524320 | tf_op jit(solution)/shard_map/ppermute | solution.py:194
  103.7 0.2 fusion.9
  104.0 0.7 fusion.28
  104.7 0.1 fusion.19
  104.8 1.9 %collective-permute-start.13 = (bf16[2,512,128]{2,1,0:T(8,128)(2,1)S(1)}, bf16[2,512,128]{2,1,0:T(8,128)(2,1)}, u32[]{:S(2)}, u32[]{:S(2)}) collective-permute-start(bf16[2,512,128]{2,1,0:T(8,128)(2,1)S(1)} %get-tuple-element.82), channel_id=1, source_target_pairs={{4,0},{6,2},{8,4},{10,6},{12,8},{14,10},{16,12},{18,14},{20,16},{2... | collective-permute-start | bytes 786440 | tf_op jit(solution)/shard_map/ppermute | solution.py:194
  106.8 1.2 collective-permute-start.14
  108.0 1.9 %collective-permute-start.16 = (bf16[2,512,128]{2,1,0:T(8,128)(2,1)S(1)}, bf16[2,512,128]{2,1,0:T(8,128)(2,1)S(1)}, u32[]{:S(2)}, u32[]{:S(2)}) collective-permute-start(bf16[2,512,128]{2,1,0:T(8,128)(2,1)S(1)} %get-tuple-element.81), channel_id=1, source_target_pairs={{4,0},{6,2},{8,4},{10,6},{12,8},{14,10},{16,12},{18,14},{20,16},{2... | collective-permute-start | bytes 786440 | tf_op jit(solution)/shard_map/ppermute | solution.py:194
  109.9 7.1 %collective-permute-done.13 = bf16[2,512,128]{2,1,0:T(8,128)(2,1)} collective-permute-done((bf16[2,512,128]{2,1,0:T(8,128)(2,1)S(1)}, bf16[2,512,128]{2,1,0:T(8,128)(2,1)}, u32[]{:S(2)}, u32[]{:S(2)}) %collective-permute-start.13) | collective-permute-done | bytes 262176 | tf_op jit(solution)/shard_map/ppermute | solution.py:194
  117.0 1.1 fusion.12
  118.0 1.2 collective-permute-start.15
  119.2 0.0 collective-permute-done.10
  119.2 0.3 broadcast_in_dim.64
  119.5 0.1 constant_dynamic-update-slice_fusion.6
  119.6 0.1 constant_dynamic-update-slice_fusion.5
  119.7 1.1 collective-permute-done.16
  120.8 0.1 constant_dynamic-update-slice_fusion.4
  120.9 0.1 constant_dynamic-update-slice_fusion.3
  121.0 3.5 %collective-permute-done.15 = bf16[2,512,128]{2,1,0:T(8,128)(2,1)S(1)} collective-permute-done((bf16[2,512,128]{2,1,0:T(8,128)(2,1)S(1)}, bf16[2,512,128]{2,1,0:T(8,128)(2,1)S(1)}, u32[]{:S(2)}, u32[]{:S(2)}) %collective-permute-start.15) | collective-permute-done | bytes 262176 | tf_op jit(solution)/shard_map/ppermute | solution.py:199
  124.5 0.1 constant_dynamic-update-slice_fusion.2
  124.6 0.2 fusion.20
  124.7 0.0 copy-start.2
  124.7 1.3 %copy-done.2 = bf16[2,512,1024]{2,1,0:T(8,128)(2,1)} copy-done((bf16[2,512,1024]{2,1,0:T(8,128)(2,1)}, bf16[2,512,1024]{2,1,0:T(8,128)(2,1)S(1)}, u32[]{:S(2)}) %copy-start.2) | copy-done | bytes 2097176
  (11 shorter events, 0.1 us)
Async XLA Ops:
  0.6 7.3 %copy-start.3 = (s32[16,2]{0,1:T(2,128)S(1)}, s32[16,2]{0,1:T(2,128)}, u32[]{:S(2)}) copy-start(s32[16,2]{0,1:T(2,128)} %param.8) | copy-start | bytes 388
  0.6 7.3 %copy-start.4 = (s32[16]{0:T(128)S(1)}, s32[16]{0:T(128)}, u32[]{:S(2)}) copy-start(s32[16]{0:T(128)} %param.9) | copy-start | bytes 196
  1.8 13.7 %collective-permute-start = (bf16[2,512,256]{2,1,0:T(8,128)(2,1)S(1)}, bf16[2,512,256]{2,1,0:T(8,128)(2,1)S(1)}, u32[]{:S(2)}, u32[]{:S(2)}) collective-permute-start(bf16[2,512,256]{2,1,0:T(8,128)(2,1)S(1)} %constant_dynamic-slice_fusion.3), channel_id=1, source_target_pairs={{0,1},{1,0},{2,3},{3,2},{4,5},{5,4},{6,7},{7,6},{8,9},{9,8},{10,11... | collective-permute-start | bytes 1572872 | tf_op jit(solution)/shard_map/ppermute | solution.py:199
  4.4 16.1 %collective-permute-start.1 = (bf16[2,512,256]{2,1,0:T(8,128)(2,1)S(1)}, bf16[2,512,256]{2,1,0:T(8,128)(2,1)S(1)}, u32[]{:S(2)}, u32[]{:S(2)}) collective-permute-start(bf16[2,512,256]{2,1,0:T(8,128)(2,1)S(1)} %constant_dynamic-slice_fusion.2.refs_4_), channel_id=1, source_target_pairs={{0,4},{2,6},{4,8},{6,10},{8,12},{10,14},{12,16},{14,18},{16,20},{1... | collective-permute-start | bytes 1572872 | tf_op jit(solution)/shard_map/ppermute | solution.py:194
  15.5 15.4 %collective-permute-start.2 = (bf16[2,512,256]{2,1,0:T(8,128)(2,1)S(1)}, bf16[2,512,256]{2,1,0:T(8,128)(2,1)S(1)}, u32[]{:S(2)}, u32[]{:S(2)}) collective-permute-start(bf16[2,512,256]{2,1,0:T(8,128)(2,1)S(1)} %collective-permute-done.refs_5_), channel_id=1, source_target_pairs={{0,4},{2,6},{4,8},{6,10},{8,12},{10,14},{12,16},{14,18},{16,20},{1... | collective-permute-start | bytes 1572872 | tf_op jit(solution)/shard_map/ppermute | solution.py:194
  18.9 12.8 %collective-permute-start.3 = (bf16[2,512,256]{2,1,0:T(8,128)(2,1)}, bf16[2,512,256]{2,1,0:T(8,128)(2,1)S(1)}, u32[]{:S(2)}, u32[]{:S(2)}) collective-permute-start(bf16[2,512,256]{2,1,0:T(8,128)(2,1)} %get-tuple-element.40), channel_id=1, source_target_pairs={{0,1},{1,0},{2,3},{3,2},{4,5},{5,4},{6,7},{7,6},{8,9},{9,8},{10,11... | collective-permute-start | bytes 1572872 | tf_op jit(solution)/shard_map/ppermute | solution.py:199
  31.0 5.5 %copy-start = (bf16[128,4096]{1,0:T(8,128)(2,1)S(1)}, bf16[128,4096]{1,0:T(8,128)(2,1)}, u32[]{:S(2)}) copy-start(bf16[128,4096]{1,0:T(8,128)(2,1)} %refs_2_.5) | copy-start | bytes 3145732
  31.0 5.5 %copy-start.1 = (bf16[128,4096]{1,0:T(8,128)(2,1)S(1)}, bf16[128,4096]{1,0:T(8,128)(2,1)}, u32[]{:S(2)}) copy-start(bf16[128,4096]{1,0:T(8,128)(2,1)} %refs_3_.5) | copy-start | bytes 3145732
  31.8 4.7 %collective-permute-start.4 = (bf16[2,1024,256]{2,1,0:T(8,128)(2,1)S(1)}, bf16[2,1024,256]{2,1,0:T(8,128)(2,1)S(1)}, u32[]{:S(2)}, u32[]{:S(2)}) collective-permute-start(bf16[2,1024,256]{2,1,0:T(8,128)(2,1)S(1)} %pad_maximum_fusion), channel_id=1, source_target_pairs={{0,2},{2,0},{4,6},{6,4},{8,10},{10,8},{12,14},{14,12},{16,18},{18,... | collective-permute-start | bytes 3145736 | tf_op jit(solution)/shard_map/ppermute | solution.py:203
  32.0 29.7 %collective-permute-start.6 = (bf16[2,1024,256]{2,1,0:T(8,128)(2,1)S(1)}, bf16[2,1024,256]{2,1,0:T(8,128)(2,1)S(1)}, u32[]{:S(2)}, u32[]{:S(2)}) collective-permute-start(bf16[2,1024,256]{2,1,0:T(8,128)(2,1)S(1)} %constant_dynamic-update-slice_fusion.refs_4_), channel_id=1, source_target_pairs={{0,4},{2,6},{4,8},{6,10},{8,12},{10,14},{12,16},{14,18},{16,20},{1... | collective-permute-start | bytes 3145736 | tf_op jit(solution)/shard_map/ppermute | solution.py:194
  61.6 2.7 %collective-permute-start.5 = (bf16[2,1024,256]{2,1,0:T(8,128)(2,1)S(1)}, bf16[2,1024,256]{2,1,0:T(8,128)(2,1)S(1)}, u32[]{:S(2)}, u32[]{:S(2)}) collective-permute-start(bf16[2,1024,256]{2,1,0:T(8,128)(2,1)S(1)} %get-tuple-element.44), channel_id=1, source_target_pairs={{0,2},{2,0},{4,6},{6,4},{8,10},{10,8},{12,14},{14,12},{16,18},{18,... | collective-permute-start | bytes 3145736 | tf_op jit(solution)/shard_map/ppermute | solution.py:203
  61.7 4.7 %collective-permute-start.7 = (bf16[2,1024,256]{2,1,0:T(8,128)(2,1)S(1)}, bf16[2,1024,256]{2,1,0:T(8,128)(2,1)S(1)}, u32[]{:S(2)}, u32[]{:S(2)}) collective-permute-start(bf16[2,1024,256]{2,1,0:T(8,128)(2,1)S(1)} %broadcast_select_fusion), channel_id=1, source_target_pairs={{0,2},{2,0},{4,6},{6,4},{8,10},{10,8},{12,14},{14,12},{16,18},{18,... | collective-permute-start | bytes 3145736 | tf_op jit(solution)/shard_map/ppermute | solution.py:203
  64.5 32.5 %collective-permute-start.9 = (bf16[2,1024,256]{2,1,0:T(8,128)(2,1)S(1)}, bf16[2,1024,256]{2,1,0:T(8,128)(2,1)S(1)}, u32[]{:S(2)}, u32[]{:S(2)}) collective-permute-start(bf16[2,1024,256]{2,1,0:T(8,128)(2,1)S(1)} %fusion.1), channel_id=1, source_target_pairs={{4,0},{6,2},{8,4},{10,6},{12,8},{14,10},{16,12},{18,14},{20,16},{2... | collective-permute-start | bytes 3145736 | tf_op jit(solution)/shard_map/ppermute | solution.py:194
  79.7 1.9 %collective-permute-start.8 = (bf16[2,1024,128]{2,1,0:T(8,128)(2,1)S(1)}, bf16[2,1024,128]{2,1,0:T(8,128)(2,1)S(1)}, u32[]{:S(2)}, u32[]{:S(2)}) collective-permute-start(bf16[2,1024,128]{2,1,0:T(8,128)(2,1)S(1)} %get-tuple-element.52), channel_id=1, source_target_pairs={{0,2},{2,0},{4,6},{6,4},{8,10},{10,8},{12,14},{14,12},{16,18},{18,... | collective-permute-start | bytes 1572872 | tf_op jit(solution)/shard_map/ppermute | solution.py:203
  81.8 22.0 %collective-permute-start.12 = (bf16[2,1024,128]{2,1,0:T(8,128)(2,1)S(1)}, bf16[2,1024,128]{2,1,0:T(8,128)(2,1)S(1)}, u32[]{:S(2)}, u32[]{:S(2)}) collective-permute-start(bf16[2,1024,128]{2,1,0:T(8,128)(2,1)S(1)} %fusion.6), channel_id=1, source_target_pairs={{4,0},{6,2},{8,4},{10,6},{12,8},{14,10},{16,12},{18,14},{20,16},{2... | collective-permute-start | bytes 1572872 | tf_op jit(solution)/shard_map/ppermute | solution.py:194
  98.2 21.0 %collective-permute-start.10 = (bf16[2,512,256]{2,1,0:T(8,128)(2,1)}, bf16[2,512,256]{2,1,0:T(8,128)(2,1)S(1)}, u32[]{:S(2)}, u32[]{:S(2)}) collective-permute-start(bf16[2,512,256]{2,1,0:T(8,128)(2,1)} %get-tuple-element.84), channel_id=1, source_target_pairs={{0,1},{1,0},{2,3},{3,2},{4,5},{5,4},{6,7},{7,6},{8,9},{9,8},{10,11... | collective-permute-start | bytes 1572872 | tf_op jit(solution)/shard_map/ppermute | solution.py:199
  99.3 5.3 %collective-permute-start.11 = (bf16[2,1024,128]{2,1,0:T(8,128)(2,1)S(1)}, bf16[2,1024,128]{2,1,0:T(8,128)(2,1)S(1)}, u32[]{:S(2)}, u32[]{:S(2)}) collective-permute-start(bf16[2,1024,128]{2,1,0:T(8,128)(2,1)S(1)} %get-tuple-element.62), channel_id=1, source_target_pairs={{0,2},{2,0},{4,6},{6,4},{8,10},{10,8},{12,14},{14,12},{16,18},{18,... | collective-permute-start | bytes 1572872 | tf_op jit(solution)/shard_map/ppermute | solution.py:203
  104.8 12.1 %collective-permute-start.13 = (bf16[2,512,128]{2,1,0:T(8,128)(2,1)S(1)}, bf16[2,512,128]{2,1,0:T(8,128)(2,1)}, u32[]{:S(2)}, u32[]{:S(2)}) collective-permute-start(bf16[2,512,128]{2,1,0:T(8,128)(2,1)S(1)} %get-tuple-element.82), channel_id=1, source_target_pairs={{4,0},{6,2},{8,4},{10,6},{12,8},{14,10},{16,12},{18,14},{20,16},{2... | collective-permute-start | bytes 786440 | tf_op jit(solution)/shard_map/ppermute | solution.py:194
  106.8 12.8 %collective-permute-start.14 = (bf16[2,512,128]{2,1,0:T(8,128)(2,1)}, bf16[2,512,128]{2,1,0:T(8,128)(2,1)S(1)}, u32[]{:S(2)}, u32[]{:S(2)}) collective-permute-start(bf16[2,512,128]{2,1,0:T(8,128)(2,1)} %get-tuple-element.85), channel_id=1, source_target_pairs={{0,1},{1,0},{2,3},{3,2},{4,5},{5,4},{6,7},{7,6},{8,9},{9,8},{10,11... | collective-permute-start | bytes 786440 | tf_op jit(solution)/shard_map/ppermute | solution.py:199
  108.0 12.8 %collective-permute-start.16 = (bf16[2,512,128]{2,1,0:T(8,128)(2,1)S(1)}, bf16[2,512,128]{2,1,0:T(8,128)(2,1)S(1)}, u32[]{:S(2)}, u32[]{:S(2)}) collective-permute-start(bf16[2,512,128]{2,1,0:T(8,128)(2,1)S(1)} %get-tuple-element.81), channel_id=1, source_target_pairs={{4,0},{6,2},{8,4},{10,6},{12,8},{14,10},{16,12},{18,14},{20,16},{2... | collective-permute-start | bytes 786440 | tf_op jit(solution)/shard_map/ppermute | solution.py:194
  118.0 6.4 %collective-permute-start.15 = (bf16[2,512,128]{2,1,0:T(8,128)(2,1)S(1)}, bf16[2,512,128]{2,1,0:T(8,128)(2,1)S(1)}, u32[]{:S(2)}, u32[]{:S(2)}) collective-permute-start(bf16[2,512,128]{2,1,0:T(8,128)(2,1)S(1)} %fusion.12), channel_id=1, source_target_pairs={{0,1},{1,0},{2,3},{3,2},{4,5},{5,4},{6,7},{7,6},{8,9},{9,8},{10,11... | collective-permute-start | bytes 786440 | tf_op jit(solution)/shard_map/ppermute | solution.py:199
  124.7 1.3 %copy-start.2 = (bf16[2,512,1024]{2,1,0:T(8,128)(2,1)}, bf16[2,512,1024]{2,1,0:T(8,128)(2,1)S(1)}, u32[]{:S(2)}) copy-start(bf16[2,512,1024]{2,1,0:T(8,128)(2,1)S(1)} %fusion.20) | copy-start | bytes 6291460

commit v2 on v1

--- a/solution.py
+++ b/solution.py
@@ -299,7 +299,7 @@
 
     for g, group in enumerate(groups):
         last = g + 1 == len(groups)
-        split = last
+        split = g > 0
         cuts = pieces if split else whole
         text, grads = attend(
             after(spans, hold),
@@ -321,7 +321,7 @@
         if last and len(pending) > 0:
             more, waited = finish(pending.pop(0), near_grad)
             placed += more
-            near_back = after(near_back, waited)
+            near_back = after(near_back, waited[-1])
         if g == 0 and len(arrivals) > 1:
             next_own, next_far = after((next_own, next_far), near_grad)
             kv = [[next_own], [exchanged(jnp.where(odd, next_far, next_own), "seq")], [next_far]]

time: 127 us -> 130 us (1.024); the launches traced: 126 us -> 128 us
  starting transfers between devices: 25.7 us -> 28.1 us
    ppermute x7 -> x8, waiting for transfers between devices: 21.8 us -> 18.5 us  [shifted(): return lax.ppermute(shard, axis, pairs)]
    ppermute x5, waiting for transfers between devices: 4.83 us -> 7.45 us  [rotated(): lax.ppermute(shard, axis, [(i, (i + by) % count) for i in range(count)])]
    ppermute x7 -> x8, starting transfers between devices: 18.4 us -> 20.3 us  [shifted(): return lax.ppermute(shard, axis, pairs)]
  transfers between devices with their start and end apart: 17 -> 18, of which waited for: 9 -> 9; matrix products, arithmetic and copies ran while one was open for 8% -> 8% of each run, Pallas kernels for 41% -> 41%
where the time goes in v2:
time: 130 us; the launch traced here: 128 us
  Pallas kernels  51.7 us (40%)
  waiting for transfers between devices  29.7 us (23%)
  starting transfers between devices  28.1 us (22%)
  local copies, waits for them, and re-layouts  7.23 us (6%)
  between operations  5.53 us (4%)
  other arithmetic  5.3 us (4%)
    pallas_call x3, Pallas kernels, attend(): pl.pallas_call(functools.partial(attend_kernel, sizes, len(carried), (hea...  51.7 us
    ppermute x8, starting transfers between devices, shifted(): return lax.ppermute(shard, axis, pairs)  20.3 us
    ppermute x8, waiting for transfers between devices, shifted(): return lax.ppermute(shard, axis, pairs)  18.5 us
    ppermute x5, waiting for transfers between devices, rotated(): lax.ppermute(shard, axis, [(i, (i + by) % count) for i in range(count)])  7.45 us
    ppermute x5, starting transfers between devices, rotated(): lax.ppermute(shard, axis, [(i, (i + by) % count) for i in range(count)])  6.85 us
    dynamic_slice x3, local copies, waits for them, and re-layouts, columns(): return lax.dynamic_slice_in_dim(source, start, count * HD, axis=2)  4.23 us
    ppermute x5, waiting for transfers between devices, exchanged(): lax.ppermute(shard, axis, [(i, i ^ 1) for i in range(lax.axis_size(axis))])  3.75 us
  transfers between devices with their start and end apart: 18, of which 9 were waited for; matrix products, arithmetic and copies ran while one was open for 8% of the time, Pallas kernels for 41%

profile of v2, /device:TPU:2, one launch (start us, length us, event | category | flops | bytes accessed | tf_op | source)
XLA Modules:
  0.0 127.5 jit_solution(1418418560077090275)
XLA Ops:
  0.7 1.1 constant_dynamic-slice_fusion.3
  1.8 1.6 %collective-permute-start = (bf16[2,512,256]{2,1,0:T(8,128)(2,1)S(1)}, bf16[2,512,256]{2,1,0:T(8,128)(2,1)S(1)}, u32[]{:S(2)}, u32[]{:S(2)}) collective-permute-start(bf16[2,512,256]{2,1,0:T(8,128)(2,1)S(1)} %constant_dynamic-slice_fusion.3), channel_id=1, source_target_pairs={{0,1},{1,0},{2,3},{3,2},{4,5},{5,4},{6,7},{7,6},{8,9},{9,8},{10,11... | collective-permute-start | bytes 1572872 | tf_op jit(solution)/shard_map/ppermute | solution.py:199
  3.3 1.1 constant_dynamic-slice_fusion.2.refs_4_
  4.4 3.5 %collective-permute-start.1 = (bf16[2,512,256]{2,1,0:T(8,128)(2,1)S(1)}, bf16[2,512,256]{2,1,0:T(8,128)(2,1)S(1)}, u32[]{:S(2)}, u32[]{:S(2)}) collective-permute-start(bf16[2,512,256]{2,1,0:T(8,128)(2,1)S(1)} %constant_dynamic-slice_fusion.2.refs_4_), channel_id=1, source_target_pairs={{0,4},{2,6},{4,8},{6,10},{8,12},{10,14},{12,16},{14,18},{16,20},{1... | collective-permute-start | bytes 1572872 | tf_op jit(solution)/shard_map/ppermute | solution.py:194
  7.9 0.1 select_reduce_fusion
  8.0 0.7 fusion.30
  12.6 0.1 stack.27.refs_0_
  12.7 2.1 %constant_dynamic-slice_fusion = (bf16[2,512,256]{2,1,0:T(8,128)(2,1)}, bf16[2,512,256]{2,1,0:T(8,128)(2,1)S(1)}) fusion(bf16[2,512,1024]{2,1,0:T(8,128)(2,1)} %param.7, s32[]{:T(128)S(6)} %select_n.164, s32[]{:T(128)S(6)} %select_n.163), kind=kLoop, calls=%fused_computation.50 | loop fusion | bytes 2097160 | tf_op jit(solution)/shard_map/dynamic_slice | solution.py:244
  14.8 0.7 collective-permute-done.refs_5_
  15.5 3.4 %collective-permute-start.2 = (bf16[2,512,256]{2,1,0:T(8,128)(2,1)S(1)}, bf16[2,512,256]{2,1,0:T(8,128)(2,1)S(1)}, u32[]{:S(2)}, u32[]{:S(2)}) collective-permute-start(bf16[2,512,256]{2,1,0:T(8,128)(2,1)S(1)} %collective-permute-done.refs_5_), channel_id=1, source_target_pairs={{0,4},{2,6},{4,8},{6,10},{8,12},{10,14},{12,16},{14,18},{16,20},{1... | collective-permute-start | bytes 1572872 | tf_op jit(solution)/shard_map/ppermute | solution.py:194
  18.9 1.6 %collective-permute-start.3 = (bf16[2,512,256]{2,1,0:T(8,128)(2,1)}, bf16[2,512,256]{2,1,0:T(8,128)(2,1)S(1)}, u32[]{:S(2)}, u32[]{:S(2)}) collective-permute-start(bf16[2,512,256]{2,1,0:T(8,128)(2,1)} %get-tuple-element.41), channel_id=1, source_target_pairs={{0,1},{1,0},{2,3},{3,2},{4,5},{5,4},{6,7},{7,6},{8,9},{9,8},{10,11... | collective-permute-start | bytes 1572872 | tf_op jit(solution)/shard_map/ppermute | solution.py:199
  20.5 1.2 broadcast_select_fusion.2
  21.7 9.2 %collective-permute-done.2.refs_8_ = bf16[2,512,256]{2,1,0:T(8,128)(2,1)S(1)} collective-permute-done((bf16[2,512,256]{2,1,0:T(8,128)(2,1)S(1)}, bf16[2,512,256]{2,1,0:T(8,128)(2,1)S(1)}, u32[]{:S(2)}, u32[]{:S(2)}) %collective-permute-start.2) | collective-permute-done | bytes 524320 | tf_op jit(solution)/shard_map/ppermute | solution.py:194
  30.9 0.1 broadcast_select_fusion.1
  31.0 0.0 copy-start
  31.0 0.0 copy-start.1
  31.0 0.7 collective-permute-done.3
  31.7 0.1 pad_maximum_fusion
  31.8 0.1 collective-permute-start.4
  32.0 3.8 %collective-permute-start.6 = (bf16[2,1024,256]{2,1,0:T(8,128)(2,1)S(1)}, bf16[2,1024,256]{2,1,0:T(8,128)(2,1)S(1)}, u32[]{:S(2)}, u32[]{:S(2)}) collective-permute-start(bf16[2,1024,256]{2,1,0:T(8,128)(2,1)S(1)} %constant_dynamic-update-slice_fusion.refs_4_), channel_id=1, source_target_pairs={{0,4},{2,6},{4,8},{6,10},{8,12},{10,14},{12,16},{14,18},{16,20},{1... | collective-permute-start | bytes 3145736 | tf_op jit(solution)/shard_map/ppermute | solution.py:194
  36.5 0.0 collective-permute-done.4.refs_6_
  36.5 25.1 %shard_map.85 = (bf16[128,4096]{1,0:T(8,128)(2,1)}, bf16[128,4096]{1,0:T(8,128)(2,1)}, f32[2,1024,256]{2,1,0:T(8,128)S(1)}, bf16[2,1024,256]{2,1,0:T(8,128)(2,1)S(1)}, f32[2,1024,256]{2,1,0:T(8,128)S(1)}) custom-call(s32[6]{0:T(128)S(1)} %stack.27.refs_0_, f32[1]{0:T(128)S(6)} %tanh.3.refs_1_, bf16[128,4096]{1,0:T(8,128)(2,1)S(1)} %copy-done, ...), custom_call_target="tpu_custom_call" | custom-call | flops 1 | bytes 1 | tf_op jit(solution)/shard_map/pallas_call | solution.py:165
  61.6 0.1 collective-permute-start.5
  61.7 0.0 collective-permute-done.6.refs_6_
  61.7 0.1 broadcast_select_fusion
  61.8 0.5 collective-permute-start.7
  62.3 2.0 %collective-permute-done.5 = bf16[2,1024,256]{2,1,0:T(8,128)(2,1)S(1)} collective-permute-done((bf16[2,1024,256]{2,1,0:T(8,128)(2,1)S(1)}, bf16[2,1024,256]{2,1,0:T(8,128)(2,1)S(1)}, u32[]{:S(2)}, u32[]{:S(2)}) %collective-permute-start.5) | collective-permute-done | bytes 1048608 | tf_op jit(solution)/shard_map/ppermute | solution.py:203
  64.3 0.2 fusion.1
  64.5 1.9 %collective-permute-start.9 = (bf16[2,1024,256]{2,1,0:T(8,128)(2,1)S(1)}, bf16[2,1024,256]{2,1,0:T(8,128)(2,1)S(1)}, u32[]{:S(2)}, u32[]{:S(2)}) collective-permute-start(bf16[2,1024,256]{2,1,0:T(8,128)(2,1)S(1)} %fusion.1), channel_id=1, source_target_pairs={{4,0},{6,2},{8,4},{10,6},{12,8},{14,10},{16,12},{18,14},{20,16},{2... | collective-permute-start | bytes 3145736 | tf_op jit(solution)/shard_map/ppermute | solution.py:194
  66.4 0.0 collective-permute-done.7.refs_5_
  66.5 13.2 %shard_map.86 = (bf16[128,4096]{1,0:T(8,128)(2,1)}, bf16[128,4096]{1,0:T(8,128)(2,1)}, f32[2,1024,128]{2,1,0:T(8,128)S(1)}, bf16[2,1024,128]{2,1,0:T(8,128)(2,1)S(1)}, f32[2,1024,128]{2,1,0:T(8,128)S(1)}) custom-call(s32[6]{0:T(128)S(1)} %stack.27.refs_0_, f32[1]{0:T(128)S(6)} %tanh.3.refs_1_, ...), custom_call_target="tpu_custom_call", output_to_operand_aliasing={{0}: (7, {}), {1}: (8, {})} | custom-call | flops 1 | bytes 1 | tf_op jit(solution)/shard_map/pallas_call | solution.py:165
  79.7 0.1 collective-permute-start.8
  79.8 1.8 %collective-permute-done.8 = bf16[2,1024,128]{2,1,0:T(8,128)(2,1)S(1)} collective-permute-done((bf16[2,1024,128]{2,1,0:T(8,128)(2,1)S(1)}, bf16[2,1024,128]{2,1,0:T(8,128)(2,1)S(1)}, u32[]{:S(2)}, u32[]{:S(2)}) %collective-permute-start.8) | collective-permute-done | bytes 524320 | tf_op jit(solution)/shard_map/ppermute | solution.py:203
  81.6 0.1 fusion.11
  81.8 1.9 %collective-permute-start.12 = (bf16[2,512,128]{2,1,0:T(8,128)(2,1)S(1)}, bf16[2,512,128]{2,1,0:T(8,128)(2,1)S(1)}, u32[]{:S(2)}, u32[]{:S(2)}) collective-permute-start(bf16[2,512,128]{2,1,0:T(8,128)(2,1)S(1)} %get-tuple-element.88), channel_id=1, source_target_pairs={{4,0},{6,2},{8,4},{10,6},{12,8},{14,10},{16,12},{18,14},{20,16},{2... | collective-permute-start | bytes 786440 | tf_op jit(solution)/shard_map/ppermute | solution.py:194
  83.7 1.9 %collective-permute-start.15 = (bf16[2,512,128]{2,1,0:T(8,128)(2,1)S(1)}, bf16[2,512,128]{2,1,0:T(8,128)(2,1)S(1)}, u32[]{:S(2)}, u32[]{:S(2)}) collective-permute-start(bf16[2,512,128]{2,1,0:T(8,128)(2,1)S(1)} %get-tuple-element.87), channel_id=1, source_target_pairs={{4,0},{6,2},{8,4},{10,6},{12,8},{14,10},{16,12},{18,14},{20,16},{2... | collective-permute-start | bytes 786440 | tf_op jit(solution)/shard_map/ppermute | solution.py:194
  85.6 13.3 %shard_map.87 = (bf16[128,4096]{1,0:T(8,128)(2,1)}, bf16[128,4096]{1,0:T(8,128)(2,1)}, f32[2,1024,128]{2,1,0:T(8,128)S(1)}, bf16[2,1024,128]{2,1,0:T(8,128)(2,1)S(1)}, f32[2,1024,128]{2,1,0:T(8,128)S(1)}) custom-call(s32[6]{0:T(128)S(1)} %stack.27.refs_0_, f32[1]{0:T(128)S(6)} %tanh.3.refs_1_, ...), custom_call_target="tpu_custom_call", output_to_operand_aliasing={{0}: (7, {}), {1}: (8, {})} | custom-call | flops 1 | bytes 1 | tf_op jit(solution)/shard_map/pallas_call | solution.py:165
  98.9 0.4 fusion.4
  99.3 0.9 fusion.32
  100.2 0.1 collective-permute-start.11
  100.3 1.2 collective-permute-start.10
  101.5 0.0 collective-permute-done.12
  101.5 2.3 %collective-permute-done.15 = bf16[2,512,128]{2,1,0:T(8,128)(2,1)S(1)} collective-permute-done((bf16[2,512,128]{2,1,0:T(8,128)(2,1)S(1)}, bf16[2,512,128]{2,1,0:T(8,128)(2,1)S(1)}, u32[]{:S(2)}, u32[]{:S(2)}) %collective-permute-start.15) | collective-permute-done | bytes 262176 | tf_op jit(solution)/shard_map/ppermute | solution.py:194
  103.7 0.9 fusion.14
  104.7 0.0 collective-permute-done.11
  104.7 0.1 fusion.24
  104.8 1.9 %collective-permute-start.13 = (bf16[2,512,128]{2,1,0:T(8,128)(2,1)S(1)}, bf16[2,512,128]{2,1,0:T(8,128)(2,1)}, u32[]{:S(2)}, u32[]{:S(2)}) collective-permute-start(bf16[2,512,128]{2,1,0:T(8,128)(2,1)S(1)} %get-tuple-element.84), channel_id=1, source_target_pairs={{4,0},{6,2},{8,4},{10,6},{12,8},{14,10},{16,12},{18,14},{20,16},{2... | collective-permute-start | bytes 786440 | tf_op jit(solution)/shard_map/ppermute | solution.py:194
  106.8 1.2 collective-permute-start.14
  108.0 1.9 %collective-permute-start.17 = (bf16[2,512,128]{2,1,0:T(8,128)(2,1)S(1)}, bf16[2,512,128]{2,1,0:T(8,128)(2,1)S(1)}, u32[]{:S(2)}, u32[]{:S(2)}) collective-permute-start(bf16[2,512,128]{2,1,0:T(8,128)(2,1)S(1)} %get-tuple-element.83), channel_id=1, source_target_pairs={{4,0},{6,2},{8,4},{10,6},{12,8},{14,10},{16,12},{18,14},{20,16},{2... | collective-permute-start | bytes 786440 | tf_op jit(solution)/shard_map/ppermute | solution.py:194
  110.0 7.0 %collective-permute-done.13 = bf16[2,512,128]{2,1,0:T(8,128)(2,1)} collective-permute-done((bf16[2,512,128]{2,1,0:T(8,128)(2,1)S(1)}, bf16[2,512,128]{2,1,0:T(8,128)(2,1)}, u32[]{:S(2)}, u32[]{:S(2)}) %collective-permute-start.13) | collective-permute-done | bytes 262176 | tf_op jit(solution)/shard_map/ppermute | solution.py:194
  117.0 1.1 fusion.17
  118.0 1.2 collective-permute-start.16
  119.3 0.0 collective-permute-done.10
  119.3 0.3 broadcast_in_dim.62
  119.5 0.1 constant_dynamic-update-slice_fusion.6
  119.6 0.1 constant_dynamic-update-slice_fusion.5
  119.7 1.2 collective-permute-done.14
  120.9 0.1 constant_dynamic-update-slice_fusion.4
  121.0 0.1 constant_dynamic-update-slice_fusion.3
  121.1 4.9 %collective-permute-done.16 = bf16[2,512,128]{2,1,0:T(8,128)(2,1)S(1)} collective-permute-done((bf16[2,512,128]{2,1,0:T(8,128)(2,1)S(1)}, bf16[2,512,128]{2,1,0:T(8,128)(2,1)S(1)}, u32[]{:S(2)}, u32[]{:S(2)}) %collective-permute-start.16) | collective-permute-done | bytes 262176 | tf_op jit(solution)/shard_map/ppermute | solution.py:199
  125.9 0.1 constant_dynamic-update-slice_fusion.2
  126.0 0.2 fusion.25
  126.2 0.0 copy-start.2
  126.2 1.3 %copy-done.2 = bf16[2,512,1024]{2,1,0:T(8,128)(2,1)} copy-done((bf16[2,512,1024]{2,1,0:T(8,128)(2,1)}, bf16[2,512,1024]{2,1,0:T(8,128)(2,1)S(1)}, u32[]{:S(2)}) %copy-start.2) | copy-done | bytes 2097176
  (12 shorter events, 0.1 us)
Async XLA Ops:
  0.6 7.3 %copy-start.3 = (s32[16,2]{0,1:T(2,128)S(1)}, s32[16,2]{0,1:T(2,128)}, u32[]{:S(2)}) copy-start(s32[16,2]{0,1:T(2,128)} %param.8) | copy-start | bytes 388
  0.6 7.3 %copy-start.4 = (s32[16]{0:T(128)S(1)}, s32[16]{0:T(128)}, u32[]{:S(2)}) copy-start(s32[16]{0:T(128)} %param.9) | copy-start | bytes 196
  1.8 13.7 %collective-permute-start = (bf16[2,512,256]{2,1,0:T(8,128)(2,1)S(1)}, bf16[2,512,256]{2,1,0:T(8,128)(2,1)S(1)}, u32[]{:S(2)}, u32[]{:S(2)}) collective-permute-start(bf16[2,512,256]{2,1,0:T(8,128)(2,1)S(1)} %constant_dynamic-slice_fusion.3), channel_id=1, source_target_pairs={{0,1},{1,0},{2,3},{3,2},{4,5},{5,4},{6,7},{7,6},{8,9},{9,8},{10,11... | collective-permute-start | bytes 1572872 | tf_op jit(solution)/shard_map/ppermute | solution.py:199
  4.4 16.1 %collective-permute-start.1 = (bf16[2,512,256]{2,1,0:T(8,128)(2,1)S(1)}, bf16[2,512,256]{2,1,0:T(8,128)(2,1)S(1)}, u32[]{:S(2)}, u32[]{:S(2)}) collective-permute-start(bf16[2,512,256]{2,1,0:T(8,128)(2,1)S(1)} %constant_dynamic-slice_fusion.2.refs_4_), channel_id=1, source_target_pairs={{0,4},{2,6},{4,8},{6,10},{8,12},{10,14},{12,16},{14,18},{16,20},{1... | collective-permute-start | bytes 1572872 | tf_op jit(solution)/shard_map/ppermute | solution.py:194
  15.5 15.4 %collective-permute-start.2 = (bf16[2,512,256]{2,1,0:T(8,128)(2,1)S(1)}, bf16[2,512,256]{2,1,0:T(8,128)(2,1)S(1)}, u32[]{:S(2)}, u32[]{:S(2)}) collective-permute-start(bf16[2,512,256]{2,1,0:T(8,128)(2,1)S(1)} %collective-permute-done.refs_5_), channel_id=1, source_target_pairs={{0,4},{2,6},{4,8},{6,10},{8,12},{10,14},{12,16},{14,18},{16,20},{1... | collective-permute-start | bytes 1572872 | tf_op jit(solution)/shard_map/ppermute | solution.py:194
  18.9 12.8 %collective-permute-start.3 = (bf16[2,512,256]{2,1,0:T(8,128)(2,1)}, bf16[2,512,256]{2,1,0:T(8,128)(2,1)S(1)}, u32[]{:S(2)}, u32[]{:S(2)}) collective-permute-start(bf16[2,512,256]{2,1,0:T(8,128)(2,1)} %get-tuple-element.41), channel_id=1, source_target_pairs={{0,1},{1,0},{2,3},{3,2},{4,5},{5,4},{6,7},{7,6},{8,9},{9,8},{10,11... | collective-permute-start | bytes 1572872 | tf_op jit(solution)/shard_map/ppermute | solution.py:199
  31.0 5.5 %copy-start = (bf16[128,4096]{1,0:T(8,128)(2,1)S(1)}, bf16[128,4096]{1,0:T(8,128)(2,1)}, u32[]{:S(2)}) copy-start(bf16[128,4096]{1,0:T(8,128)(2,1)} %refs_2_.5) | copy-start | bytes 3145732
  31.0 5.5 %copy-start.1 = (bf16[128,4096]{1,0:T(8,128)(2,1)S(1)}, bf16[128,4096]{1,0:T(8,128)(2,1)}, u32[]{:S(2)}) copy-start(bf16[128,4096]{1,0:T(8,128)(2,1)} %refs_3_.5) | copy-start | bytes 3145732
  31.8 4.7 %collective-permute-start.4 = (bf16[2,1024,256]{2,1,0:T(8,128)(2,1)S(1)}, bf16[2,1024,256]{2,1,0:T(8,128)(2,1)S(1)}, u32[]{:S(2)}, u32[]{:S(2)}) collective-permute-start(bf16[2,1024,256]{2,1,0:T(8,128)(2,1)S(1)} %pad_maximum_fusion), channel_id=1, source_target_pairs={{0,2},{2,0},{4,6},{6,4},{8,10},{10,8},{12,14},{14,12},{16,18},{18,... | collective-permute-start | bytes 3145736 | tf_op jit(solution)/shard_map/ppermute | solution.py:203
  32.0 29.7 %collective-permute-start.6 = (bf16[2,1024,256]{2,1,0:T(8,128)(2,1)S(1)}, bf16[2,1024,256]{2,1,0:T(8,128)(2,1)S(1)}, u32[]{:S(2)}, u32[]{:S(2)}) collective-permute-start(bf16[2,1024,256]{2,1,0:T(8,128)(2,1)S(1)} %constant_dynamic-update-slice_fusion.refs_4_), channel_id=1, source_target_pairs={{0,4},{2,6},{4,8},{6,10},{8,12},{10,14},{12,16},{14,18},{16,20},{1... | collective-permute-start | bytes 3145736 | tf_op jit(solution)/shard_map/ppermute | solution.py:194
  61.6 2.7 %collective-permute-start.5 = (bf16[2,1024,256]{2,1,0:T(8,128)(2,1)S(1)}, bf16[2,1024,256]{2,1,0:T(8,128)(2,1)S(1)}, u32[]{:S(2)}, u32[]{:S(2)}) collective-permute-start(bf16[2,1024,256]{2,1,0:T(8,128)(2,1)S(1)} %get-tuple-element.45), channel_id=1, source_target_pairs={{0,2},{2,0},{4,6},{6,4},{8,10},{10,8},{12,14},{14,12},{16,18},{18,... | collective-permute-start | bytes 3145736 | tf_op jit(solution)/shard_map/ppermute | solution.py:203
  61.8 4.7 %collective-permute-start.7 = (bf16[2,1024,256]{2,1,0:T(8,128)(2,1)S(1)}, bf16[2,1024,256]{2,1,0:T(8,128)(2,1)S(1)}, u32[]{:S(2)}, u32[]{:S(2)}) collective-permute-start(bf16[2,1024,256]{2,1,0:T(8,128)(2,1)S(1)} %broadcast_select_fusion), channel_id=1, source_target_pairs={{0,2},{2,0},{4,6},{6,4},{8,10},{10,8},{12,14},{14,12},{16,18},{18,... | collective-permute-start | bytes 3145736 | tf_op jit(solution)/shard_map/ppermute | solution.py:203
  64.5 34.4 %collective-permute-start.9 = (bf16[2,1024,256]{2,1,0:T(8,128)(2,1)S(1)}, bf16[2,1024,256]{2,1,0:T(8,128)(2,1)S(1)}, u32[]{:S(2)}, u32[]{:S(2)}) collective-permute-start(bf16[2,1024,256]{2,1,0:T(8,128)(2,1)S(1)} %fusion.1), channel_id=1, source_target_pairs={{4,0},{6,2},{8,4},{10,6},{12,8},{14,10},{16,12},{18,14},{20,16},{2... | collective-permute-start | bytes 3145736 | tf_op jit(solution)/shard_map/ppermute | solution.py:194
  79.7 1.9 %collective-permute-start.8 = (bf16[2,1024,128]{2,1,0:T(8,128)(2,1)S(1)}, bf16[2,1024,128]{2,1,0:T(8,128)(2,1)S(1)}, u32[]{:S(2)}, u32[]{:S(2)}) collective-permute-start(bf16[2,1024,128]{2,1,0:T(8,128)(2,1)S(1)} %get-tuple-element.53), channel_id=1, source_target_pairs={{0,2},{2,0},{4,6},{6,4},{8,10},{10,8},{12,14},{14,12},{16,18},{18,... | collective-permute-start | bytes 1572872 | tf_op jit(solution)/shard_map/ppermute | solution.py:203
  81.8 19.7 %collective-permute-start.12 = (bf16[2,512,128]{2,1,0:T(8,128)(2,1)S(1)}, bf16[2,512,128]{2,1,0:T(8,128)(2,1)S(1)}, u32[]{:S(2)}, u32[]{:S(2)}) collective-permute-start(bf16[2,512,128]{2,1,0:T(8,128)(2,1)S(1)} %get-tuple-element.88), channel_id=1, source_target_pairs={{4,0},{6,2},{8,4},{10,6},{12,8},{14,10},{16,12},{18,14},{20,16},{2... | collective-permute-start | bytes 786440 | tf_op jit(solution)/shard_map/ppermute | solution.py:194
  83.7 20.1 %collective-permute-start.15 = (bf16[2,512,128]{2,1,0:T(8,128)(2,1)S(1)}, bf16[2,512,128]{2,1,0:T(8,128)(2,1)S(1)}, u32[]{:S(2)}, u32[]{:S(2)}) collective-permute-start(bf16[2,512,128]{2,1,0:T(8,128)(2,1)S(1)} %get-tuple-element.87), channel_id=1, source_target_pairs={{4,0},{6,2},{8,4},{10,6},{12,8},{14,10},{16,12},{18,14},{20,16},{2... | collective-permute-start | bytes 786440 | tf_op jit(solution)/shard_map/ppermute | solution.py:194
  100.2 4.5 %collective-permute-start.11 = (bf16[2,1024,128]{2,1,0:T(8,128)(2,1)S(1)}, bf16[2,1024,128]{2,1,0:T(8,128)(2,1)S(1)}, u32[]{:S(2)}, u32[]{:S(2)}) collective-permute-start(bf16[2,1024,128]{2,1,0:T(8,128)(2,1)S(1)} %get-tuple-element.63), channel_id=1, source_target_pairs={{0,2},{2,0},{4,6},{6,4},{8,10},{10,8},{12,14},{14,12},{16,18},{18,... | collective-permute-start | bytes 1572872 | tf_op jit(solution)/shard_map/ppermute | solution.py:203
  100.3 19.0 %collective-permute-start.10 = (bf16[2,512,256]{2,1,0:T(8,128)(2,1)}, bf16[2,512,256]{2,1,0:T(8,128)(2,1)S(1)}, u32[]{:S(2)}, u32[]{:S(2)}) collective-permute-start(bf16[2,512,256]{2,1,0:T(8,128)(2,1)} %get-tuple-element.90), channel_id=1, source_target_pairs={{0,1},{1,0},{2,3},{3,2},{4,5},{5,4},{6,7},{7,6},{8,9},{9,8},{10,11... | collective-permute-start | bytes 1572872 | tf_op jit(solution)/shard_map/ppermute | solution.py:199
  104.8 12.1 %collective-permute-start.13 = (bf16[2,512,128]{2,1,0:T(8,128)(2,1)S(1)}, bf16[2,512,128]{2,1,0:T(8,128)(2,1)}, u32[]{:S(2)}, u32[]{:S(2)}) collective-permute-start(bf16[2,512,128]{2,1,0:T(8,128)(2,1)S(1)} %get-tuple-element.84), channel_id=1, source_target_pairs={{4,0},{6,2},{8,4},{10,6},{12,8},{14,10},{16,12},{18,14},{20,16},{2... | collective-permute-start | bytes 786440 | tf_op jit(solution)/shard_map/ppermute | solution.py:194
  106.8 14.1 %collective-permute-start.14 = (bf16[2,512,128]{2,1,0:T(8,128)(2,1)}, bf16[2,512,128]{2,1,0:T(8,128)(2,1)S(1)}, u32[]{:S(2)}, u32[]{:S(2)}) collective-permute-start(bf16[2,512,128]{2,1,0:T(8,128)(2,1)} %get-tuple-element.86), channel_id=1, source_target_pairs={{0,1},{1,0},{2,3},{3,2},{4,5},{5,4},{6,7},{7,6},{8,9},{9,8},{10,11... | collective-permute-start | bytes 786440 | tf_op jit(solution)/shard_map/ppermute | solution.py:199
  108.0 12.8 %collective-permute-start.17 = (bf16[2,512,128]{2,1,0:T(8,128)(2,1)S(1)}, bf16[2,512,128]{2,1,0:T(8,128)(2,1)S(1)}, u32[]{:S(2)}, u32[]{:S(2)}) collective-permute-start(bf16[2,512,128]{2,1,0:T(8,128)(2,1)S(1)} %get-tuple-element.83), channel_id=1, source_target_pairs={{4,0},{6,2},{8,4},{10,6},{12,8},{14,10},{16,12},{18,14},{20,16},{2... | collective-permute-start | bytes 786440 | tf_op jit(solution)/shard_map/ppermute | solution.py:194
  118.0 7.9 %collective-permute-start.16 = (bf16[2,512,128]{2,1,0:T(8,128)(2,1)S(1)}, bf16[2,512,128]{2,1,0:T(8,128)(2,1)S(1)}, u32[]{:S(2)}, u32[]{:S(2)}) collective-permute-start(bf16[2,512,128]{2,1,0:T(8,128)(2,1)S(1)} %fusion.17), channel_id=1, source_target_pairs={{0,1},{1,0},{2,3},{3,2},{4,5},{5,4},{6,7},{7,6},{8,9},{9,8},{10,11... | collective-permute-start | bytes 786440 | tf_op jit(solution)/shard_map/ppermute | solution.py:199
  126.2 1.3 %copy-start.2 = (bf16[2,512,1024]{2,1,0:T(8,128)(2,1)}, bf16[2,512,1024]{2,1,0:T(8,128)(2,1)S(1)}, u32[]{:S(2)}) copy-start(bf16[2,512,1024]{2,1,0:T(8,128)(2,1)S(1)} %fusion.25) | copy-start | bytes 6291460

commit v3 on v1

--- a/solution.py
+++ b/solution.py
@@ -17,7 +17,7 @@
 BIG = 1e30
 VMEM_LIMIT = 36 * 2**20
 GRAD_TYPES = (jnp.float32, jnp.bfloat16, jnp.float32)
-BLK = 512
+BLK = 1024
 UNROLLED = 2
 NT = (((1,), (1,)), ((), ()))
 NN = (((1,), (0,)), ((), ()))

time: 127 us -> 126 us (level)
  no operation moved by 1% of the time
where the time goes in v3:
time: 126 us
  Pallas kernels  51.4 us (41%)
  waiting for transfers between devices  30.7 us (24%)
  starting transfers between devices  25.7 us (20%)
  local copies, waits for them, and re-layouts  7.96 us (6%)
  between operations  5.59 us (4%)
  other arithmetic  4.62 us (4%)
    pallas_call x3, Pallas kernels, attend(): pl.pallas_call(functools.partial(attend_kernel, sizes, len(carried), (hea...  51.4 us
    ppermute x7, waiting for transfers between devices, shifted(): return lax.ppermute(shard, axis, pairs)  22 us
    ppermute x7, starting transfers between devices, shifted(): return lax.ppermute(shard, axis, pairs)  18.4 us
    ppermute x5, starting transfers between devices, rotated(): lax.ppermute(shard, axis, [(i, (i + by) % count) for i in range(count)])  6.67 us
    ppermute x5, waiting for transfers between devices, rotated(): lax.ppermute(shard, axis, [(i, (i + by) % count) for i in range(count)])  4.83 us
    dynamic_slice x3, local copies, waits for them, and re-layouts, columns(): return lax.dynamic_slice_in_dim(source, start, count * HD, axis=2)  4.23 us
    ppermute x5, waiting for transfers between devices, exchanged(): lax.ppermute(shard, axis, [(i, i ^ 1) for i in range(lax.axis_size(axis))])  3.88 us
  transfers between devices with their start and end apart: 17, of which 9 were waited for; matrix products, arithmetic and copies ran while one was open for 8% of the time, Pallas kernels for 41%

profile of v3, /device:TPU:2, one launch (start us, length us, event | category | flops | bytes accessed | tf_op | source)
XLA Modules:
  0.0 126.0 jit_solution(11087031293063937544)
XLA Ops:
  0.7 1.1 constant_dynamic-slice_fusion.3
  1.8 1.6 %collective-permute-start = (bf16[2,512,256]{2,1,0:T(8,128)(2,1)S(1)}, bf16[2,512,256]{2,1,0:T(8,128)(2,1)S(1)}, u32[]{:S(2)}, u32[]{:S(2)}) collective-permute-start(bf16[2,512,256]{2,1,0:T(8,128)(2,1)S(1)} %constant_dynamic-slice_fusion.3), channel_id=1, source_target_pairs={{0,1},{1,0},{2,3},{3,2},{4,5},{5,4},{6,7},{7,6},{8,9},{9,8},{10,11... | collective-permute-start | bytes 1572872 | tf_op jit(solution)/shard_map/ppermute | solution.py:199
  3.3 1.1 constant_dynamic-slice_fusion.2.refs_4_
  4.4 3.5 %collective-permute-start.1 = (bf16[2,512,256]{2,1,0:T(8,128)(2,1)S(1)}, bf16[2,512,256]{2,1,0:T(8,128)(2,1)S(1)}, u32[]{:S(2)}, u32[]{:S(2)}) collective-permute-start(bf16[2,512,256]{2,1,0:T(8,128)(2,1)S(1)} %constant_dynamic-slice_fusion.2.refs_4_), channel_id=1, source_target_pairs={{0,4},{2,6},{4,8},{6,10},{8,12},{10,14},{12,16},{14,18},{16,20},{1... | collective-permute-start | bytes 1572872 | tf_op jit(solution)/shard_map/ppermute | solution.py:194
  7.9 0.1 select_reduce_fusion
  8.0 0.8 fusion.25
  12.7 0.1 stack.27.refs_0_
  12.8 2.1 %constant_dynamic-slice_fusion = (bf16[2,512,256]{2,1,0:T(8,128)(2,1)}, bf16[2,512,256]{2,1,0:T(8,128)(2,1)S(1)}) fusion(bf16[2,512,1024]{2,1,0:T(8,128)(2,1)} %param.7, s32[]{:T(128)S(6)} %select_n.162, s32[]{:T(128)S(6)} %select_n.161), kind=kLoop, calls=%fused_computation.43 | loop fusion | bytes 2097160 | tf_op jit(solution)/shard_map/dynamic_slice | solution.py:244
  14.9 0.6 collective-permute-done.refs_5_
  15.5 3.4 %collective-permute-start.2 = (bf16[2,512,256]{2,1,0:T(8,128)(2,1)S(1)}, bf16[2,512,256]{2,1,0:T(8,128)(2,1)S(1)}, u32[]{:S(2)}, u32[]{:S(2)}) collective-permute-start(bf16[2,512,256]{2,1,0:T(8,128)(2,1)S(1)} %collective-permute-done.refs_5_), channel_id=1, source_target_pairs={{0,4},{2,6},{4,8},{6,10},{8,12},{10,14},{12,16},{14,18},{16,20},{1... | collective-permute-start | bytes 1572872 | tf_op jit(solution)/shard_map/ppermute | solution.py:194
  18.9 1.6 %collective-permute-start.3 = (bf16[2,512,256]{2,1,0:T(8,128)(2,1)}, bf16[2,512,256]{2,1,0:T(8,128)(2,1)S(1)}, u32[]{:S(2)}, u32[]{:S(2)}) collective-permute-start(bf16[2,512,256]{2,1,0:T(8,128)(2,1)} %get-tuple-element.40), channel_id=1, source_target_pairs={{0,1},{1,0},{2,3},{3,2},{4,5},{5,4},{6,7},{7,6},{8,9},{9,8},{10,11... | collective-permute-start | bytes 1572872 | tf_op jit(solution)/shard_map/ppermute | solution.py:199
  20.5 0.0 collective-permute-done.1.refs_7_
  20.5 1.2 broadcast_select_fusion.2
  21.7 9.2 %collective-permute-done.2.refs_8_ = bf16[2,512,256]{2,1,0:T(8,128)(2,1)S(1)} collective-permute-done((bf16[2,512,256]{2,1,0:T(8,128)(2,1)S(1)}, bf16[2,512,256]{2,1,0:T(8,128)(2,1)S(1)}, u32[]{:S(2)}, u32[]{:S(2)}) %collective-permute-start.2) | collective-permute-done | bytes 524320 | tf_op jit(solution)/shard_map/ppermute | solution.py:194
  30.9 0.1 broadcast_select_fusion.1
  31.0 0.0 copy-start
  31.0 0.0 copy-start.1
  31.0 0.7 collective-permute-done.3
  31.7 0.1 pad_maximum_fusion
  31.8 0.1 collective-permute-start.4
  32.0 3.8 %collective-permute-start.6 = (bf16[2,1024,256]{2,1,0:T(8,128)(2,1)S(1)}, bf16[2,1024,256]{2,1,0:T(8,128)(2,1)S(1)}, u32[]{:S(2)}, u32[]{:S(2)}) collective-permute-start(bf16[2,1024,256]{2,1,0:T(8,128)(2,1)S(1)} %constant_dynamic-update-slice_fusion.refs_4_), channel_id=1, source_target_pairs={{0,4},{2,6},{4,8},{6,10},{8,12},{10,14},{12,16},{14,18},{16,20},{1... | collective-permute-start | bytes 3145736 | tf_op jit(solution)/shard_map/ppermute | solution.py:194
  36.5 0.0 collective-permute-done.4.refs_6_
  36.5 25.0 %shard_map.85 = (bf16[128,4096]{1,0:T(8,128)(2,1)}, bf16[128,4096]{1,0:T(8,128)(2,1)}, f32[2,1024,256]{2,1,0:T(8,128)S(1)}, bf16[2,1024,256]{2,1,0:T(8,128)(2,1)S(1)}, f32[2,1024,256]{2,1,0:T(8,128)S(1)}) custom-call(s32[6]{0:T(128)S(1)} %stack.27.refs_0_, f32[1]{0:T(128)S(6)} %tanh.3.refs_1_, bf16[128,4096]{1,0:T(8,128)(2,1)S(1)} %copy-done, ...), custom_call_target="tpu_custom_call" | custom-call | flops 1 | bytes 1 | tf_op jit(solution)/shard_map/pallas_call | solution.py:165
  61.5 0.0 collective-permute-start.5
  61.5 0.0 collective-permute-done.6.refs_6_
  61.5 0.1 broadcast_select_fusion
  61.7 0.6 collective-permute-start.7
  62.2 2.0 %collective-permute-done.5 = bf16[2,1024,256]{2,1,0:T(8,128)(2,1)S(1)} collective-permute-done((bf16[2,1024,256]{2,1,0:T(8,128)(2,1)S(1)}, bf16[2,1024,256]{2,1,0:T(8,128)(2,1)S(1)}, u32[]{:S(2)}, u32[]{:S(2)}) %collective-permute-start.5) | collective-permute-done | bytes 1048608 | tf_op jit(solution)/shard_map/ppermute | solution.py:203
  64.2 0.2 fusion.1
  64.4 1.9 %collective-permute-start.9 = (bf16[2,1024,256]{2,1,0:T(8,128)(2,1)S(1)}, bf16[2,1024,256]{2,1,0:T(8,128)(2,1)S(1)}, u32[]{:S(2)}, u32[]{:S(2)}) collective-permute-start(bf16[2,1024,256]{2,1,0:T(8,128)(2,1)S(1)} %fusion.1), channel_id=1, source_target_pairs={{4,0},{6,2},{8,4},{10,6},{12,8},{14,10},{16,12},{18,14},{20,16},{2... | collective-permute-start | bytes 3145736 | tf_op jit(solution)/shard_map/ppermute | solution.py:194
  66.4 0.0 collective-permute-done.7.refs_5_
  66.4 13.1 %shard_map.86 = (bf16[128,4096]{1,0:T(8,128)(2,1)}, bf16[128,4096]{1,0:T(8,128)(2,1)}, f32[2,1024,128]{2,1,0:T(8,128)S(1)}, bf16[2,1024,128]{2,1,0:T(8,128)(2,1)S(1)}, f32[2,1024,128]{2,1,0:T(8,128)S(1)}) custom-call(s32[6]{0:T(128)S(1)} %stack.27.refs_0_, f32[1]{0:T(128)S(6)} %tanh.3.refs_1_, ...), custom_call_target="tpu_custom_call", output_to_operand_aliasing={{0}: (7, {}), {1}: (8, {})} | custom-call | flops 1 | bytes 1 | tf_op jit(solution)/shard_map/pallas_call | solution.py:165
  79.5 0.0 collective-permute-start.8
  79.5 1.9 %collective-permute-done.8 = bf16[2,1024,128]{2,1,0:T(8,128)(2,1)S(1)} collective-permute-done((bf16[2,1024,128]{2,1,0:T(8,128)(2,1)S(1)}, bf16[2,1024,128]{2,1,0:T(8,128)(2,1)S(1)}, u32[]{:S(2)}, u32[]{:S(2)}) %collective-permute-start.8) | collective-permute-done | bytes 524320 | tf_op jit(solution)/shard_map/ppermute | solution.py:203
  81.4 0.1 fusion.6
  81.6 1.9 %collective-permute-start.12 = (bf16[2,1024,128]{2,1,0:T(8,128)(2,1)S(1)}, bf16[2,1024,128]{2,1,0:T(8,128)(2,1)S(1)}, u32[]{:S(2)}, u32[]{:S(2)}) collective-permute-start(bf16[2,1024,128]{2,1,0:T(8,128)(2,1)S(1)} %fusion.6), channel_id=1, source_target_pairs={{4,0},{6,2},{8,4},{10,6},{12,8},{14,10},{16,12},{18,14},{20,16},{2... | collective-permute-start | bytes 1572872 | tf_op jit(solution)/shard_map/ppermute | solution.py:194
  83.5 13.2 %shard_map.87 = (bf16[128,4096]{1,0:T(8,128)(2,1)}, bf16[128,4096]{1,0:T(8,128)(2,1)}, f32[2,1024,128]{2,1,0:T(8,128)S(1)}, bf16[2,1024,128]{2,1,0:T(8,128)(2,1)S(1)}, f32[2,1024,128]{2,1,0:T(8,128)S(1)}) custom-call(s32[6]{0:T(128)S(1)} %stack.27.refs_0_, f32[1]{0:T(128)S(6)} %tanh.3.refs_1_, ...), custom_call_target="tpu_custom_call", output_to_operand_aliasing={{0}: (7, {}), {1}: (8, {})} | custom-call | flops 1 | bytes 1 | tf_op jit(solution)/shard_map/pallas_call | solution.py:165
  96.7 0.0 collective-permute-done.9
  96.7 0.4 fusion.4
  97.1 0.9 fusion.27
  98.0 1.1 collective-permute-start.10
  99.1 4.6 %collective-permute-done.12 = bf16[2,1024,128]{2,1,0:T(8,128)(2,1)S(1)} collective-permute-done((bf16[2,1024,128]{2,1,0:T(8,128)(2,1)S(1)}, bf16[2,1024,128]{2,1,0:T(8,128)(2,1)S(1)}, u32[]{:S(2)}, u32[]{:S(2)}) %collective-permute-start.12) | collective-permute-done | bytes 524320 | tf_op jit(solution)/shard_map/ppermute | solution.py:194
  103.7 0.2 fusion.9
  103.9 0.7 fusion.28
  104.6 0.0 collective-permute-done.11
  104.6 0.1 fusion.19
  104.8 1.9 %collective-permute-start.13 = (bf16[2,512,128]{2,1,0:T(8,128)(2,1)S(1)}, bf16[2,512,128]{2,1,0:T(8,128)(2,1)}, u32[]{:S(2)}, u32[]{:S(2)}) collective-permute-start(bf16[2,512,128]{2,1,0:T(8,128)(2,1)S(1)} %get-tuple-element.82), channel_id=1, source_target_pairs={{4,0},{6,2},{8,4},{10,6},{12,8},{14,10},{16,12},{18,14},{20,16},{2... | collective-permute-start | bytes 786440 | tf_op jit(solution)/shard_map/ppermute | solution.py:194
  106.7 1.2 collective-permute-start.14
  107.9 1.9 %collective-permute-start.16 = (bf16[2,512,128]{2,1,0:T(8,128)(2,1)S(1)}, bf16[2,512,128]{2,1,0:T(8,128)(2,1)S(1)}, u32[]{:S(2)}, u32[]{:S(2)}) collective-permute-start(bf16[2,512,128]{2,1,0:T(8,128)(2,1)S(1)} %get-tuple-element.81), channel_id=1, source_target_pairs={{4,0},{6,2},{8,4},{10,6},{12,8},{14,10},{16,12},{18,14},{20,16},{2... | collective-permute-start | bytes 786440 | tf_op jit(solution)/shard_map/ppermute | solution.py:194
  109.8 7.1 %collective-permute-done.13 = bf16[2,512,128]{2,1,0:T(8,128)(2,1)} collective-permute-done((bf16[2,512,128]{2,1,0:T(8,128)(2,1)S(1)}, bf16[2,512,128]{2,1,0:T(8,128)(2,1)}, u32[]{:S(2)}, u32[]{:S(2)}) %collective-permute-start.13) | collective-permute-done | bytes 262176 | tf_op jit(solution)/shard_map/ppermute | solution.py:194
  116.9 1.1 fusion.12
  118.0 1.2 collective-permute-start.15
  119.2 0.3 broadcast_in_dim.64
  119.4 0.1 constant_dynamic-update-slice_fusion.6
  119.5 0.1 constant_dynamic-update-slice_fusion.5
  119.6 0.0 collective-permute-done.14
  119.6 1.1 collective-permute-done.16
  120.7 0.1 constant_dynamic-update-slice_fusion.4
  120.8 0.1 constant_dynamic-update-slice_fusion.3
  120.9 3.5 %collective-permute-done.15 = bf16[2,512,128]{2,1,0:T(8,128)(2,1)S(1)} collective-permute-done((bf16[2,512,128]{2,1,0:T(8,128)(2,1)S(1)}, bf16[2,512,128]{2,1,0:T(8,128)(2,1)S(1)}, u32[]{:S(2)}, u32[]{:S(2)}) %collective-permute-start.15) | collective-permute-done | bytes 262176 | tf_op jit(solution)/shard_map/ppermute | solution.py:199
  124.4 0.1 constant_dynamic-update-slice_fusion.2
  124.5 0.2 fusion.20
  124.7 0.0 copy-start.2
  124.7 1.3 %copy-done.2 = bf16[2,512,1024]{2,1,0:T(8,128)(2,1)} copy-done((bf16[2,512,1024]{2,1,0:T(8,128)(2,1)}, bf16[2,512,1024]{2,1,0:T(8,128)(2,1)S(1)}, u32[]{:S(2)}) %copy-start.2) | copy-done | bytes 2097176
  (11 shorter events, 0.1 us)
Async XLA Ops:
  0.6 7.3 %copy-start.3 = (s32[16,2]{0,1:T(2,128)S(1)}, s32[16,2]{0,1:T(2,128)}, u32[]{:S(2)}) copy-start(s32[16,2]{0,1:T(2,128)} %param.8) | copy-start | bytes 388
  0.6 7.3 %copy-start.4 = (s32[16]{0:T(128)S(1)}, s32[16]{0:T(128)}, u32[]{:S(2)}) copy-start(s32[16]{0:T(128)} %param.9) | copy-start | bytes 196
  1.8 13.7 %collective-permute-start = (bf16[2,512,256]{2,1,0:T(8,128)(2,1)S(1)}, bf16[2,512,256]{2,1,0:T(8,128)(2,1)S(1)}, u32[]{:S(2)}, u32[]{:S(2)}) collective-permute-start(bf16[2,512,256]{2,1,0:T(8,128)(2,1)S(1)} %constant_dynamic-slice_fusion.3), channel_id=1, source_target_pairs={{0,1},{1,0},{2,3},{3,2},{4,5},{5,4},{6,7},{7,6},{8,9},{9,8},{10,11... | collective-permute-start | bytes 1572872 | tf_op jit(solution)/shard_map/ppermute | solution.py:199
  4.4 16.1 %collective-permute-start.1 = (bf16[2,512,256]{2,1,0:T(8,128)(2,1)S(1)}, bf16[2,512,256]{2,1,0:T(8,128)(2,1)S(1)}, u32[]{:S(2)}, u32[]{:S(2)}) collective-permute-start(bf16[2,512,256]{2,1,0:T(8,128)(2,1)S(1)} %constant_dynamic-slice_fusion.2.refs_4_), channel_id=1, source_target_pairs={{0,4},{2,6},{4,8},{6,10},{8,12},{10,14},{12,16},{14,18},{16,20},{1... | collective-permute-start | bytes 1572872 | tf_op jit(solution)/shard_map/ppermute | solution.py:194
  15.5 15.4 %collective-permute-start.2 = (bf16[2,512,256]{2,1,0:T(8,128)(2,1)S(1)}, bf16[2,512,256]{2,1,0:T(8,128)(2,1)S(1)}, u32[]{:S(2)}, u32[]{:S(2)}) collective-permute-start(bf16[2,512,256]{2,1,0:T(8,128)(2,1)S(1)} %collective-permute-done.refs_5_), channel_id=1, source_target_pairs={{0,4},{2,6},{4,8},{6,10},{8,12},{10,14},{12,16},{14,18},{16,20},{1... | collective-permute-start | bytes 1572872 | tf_op jit(solution)/shard_map/ppermute | solution.py:194
  18.9 12.8 %collective-permute-start.3 = (bf16[2,512,256]{2,1,0:T(8,128)(2,1)}, bf16[2,512,256]{2,1,0:T(8,128)(2,1)S(1)}, u32[]{:S(2)}, u32[]{:S(2)}) collective-permute-start(bf16[2,512,256]{2,1,0:T(8,128)(2,1)} %get-tuple-element.40), channel_id=1, source_target_pairs={{0,1},{1,0},{2,3},{3,2},{4,5},{5,4},{6,7},{7,6},{8,9},{9,8},{10,11... | collective-permute-start | bytes 1572872 | tf_op jit(solution)/shard_map/ppermute | solution.py:199
  31.0 5.5 %copy-start = (bf16[128,4096]{1,0:T(8,128)(2,1)S(1)}, bf16[128,4096]{1,0:T(8,128)(2,1)}, u32[]{:S(2)}) copy-start(bf16[128,4096]{1,0:T(8,128)(2,1)} %refs_2_.5) | copy-start | bytes 3145732
  31.0 5.5 %copy-start.1 = (bf16[128,4096]{1,0:T(8,128)(2,1)S(1)}, bf16[128,4096]{1,0:T(8,128)(2,1)}, u32[]{:S(2)}) copy-start(bf16[128,4096]{1,0:T(8,128)(2,1)} %refs_3_.5) | copy-start | bytes 3145732
  31.8 4.7 %collective-permute-start.4 = (bf16[2,1024,256]{2,1,0:T(8,128)(2,1)S(1)}, bf16[2,1024,256]{2,1,0:T(8,128)(2,1)S(1)}, u32[]{:S(2)}, u32[]{:S(2)}) collective-permute-start(bf16[2,1024,256]{2,1,0:T(8,128)(2,1)S(1)} %pad_maximum_fusion), channel_id=1, source_target_pairs={{0,2},{2,0},{4,6},{6,4},{8,10},{10,8},{12,14},{14,12},{16,18},{18,... | collective-permute-start | bytes 3145736 | tf_op jit(solution)/shard_map/ppermute | solution.py:203
  32.0 29.6 %collective-permute-start.6 = (bf16[2,1024,256]{2,1,0:T(8,128)(2,1)S(1)}, bf16[2,1024,256]{2,1,0:T(8,128)(2,1)S(1)}, u32[]{:S(2)}, u32[]{:S(2)}) collective-permute-start(bf16[2,1024,256]{2,1,0:T(8,128)(2,1)S(1)} %constant_dynamic-update-slice_fusion.refs_4_), channel_id=1, source_target_pairs={{0,4},{2,6},{4,8},{6,10},{8,12},{10,14},{12,16},{14,18},{16,20},{1... | collective-permute-start | bytes 3145736 | tf_op jit(solution)/shard_map/ppermute | solution.py:194
  61.5 2.7 %collective-permute-start.5 = (bf16[2,1024,256]{2,1,0:T(8,128)(2,1)S(1)}, bf16[2,1024,256]{2,1,0:T(8,128)(2,1)S(1)}, u32[]{:S(2)}, u32[]{:S(2)}) collective-permute-start(bf16[2,1024,256]{2,1,0:T(8,128)(2,1)S(1)} %get-tuple-element.44), channel_id=1, source_target_pairs={{0,2},{2,0},{4,6},{6,4},{8,10},{10,8},{12,14},{14,12},{16,18},{18,... | collective-permute-start | bytes 3145736 | tf_op jit(solution)/shard_map/ppermute | solution.py:203
  61.7 4.7 %collective-permute-start.7 = (bf16[2,1024,256]{2,1,0:T(8,128)(2,1)S(1)}, bf16[2,1024,256]{2,1,0:T(8,128)(2,1)S(1)}, u32[]{:S(2)}, u32[]{:S(2)}) collective-permute-start(bf16[2,1024,256]{2,1,0:T(8,128)(2,1)S(1)} %broadcast_select_fusion), channel_id=1, source_target_pairs={{0,2},{2,0},{4,6},{6,4},{8,10},{10,8},{12,14},{14,12},{16,18},{18,... | collective-permute-start | bytes 3145736 | tf_op jit(solution)/shard_map/ppermute | solution.py:203
  64.4 32.3 %collective-permute-start.9 = (bf16[2,1024,256]{2,1,0:T(8,128)(2,1)S(1)}, bf16[2,1024,256]{2,1,0:T(8,128)(2,1)S(1)}, u32[]{:S(2)}, u32[]{:S(2)}) collective-permute-start(bf16[2,1024,256]{2,1,0:T(8,128)(2,1)S(1)} %fusion.1), channel_id=1, source_target_pairs={{4,0},{6,2},{8,4},{10,6},{12,8},{14,10},{16,12},{18,14},{20,16},{2... | collective-permute-start | bytes 3145736 | tf_op jit(solution)/shard_map/ppermute | solution.py:194
  79.5 1.9 %collective-permute-start.8 = (bf16[2,1024,128]{2,1,0:T(8,128)(2,1)S(1)}, bf16[2,1024,128]{2,1,0:T(8,128)(2,1)S(1)}, u32[]{:S(2)}, u32[]{:S(2)}) collective-permute-start(bf16[2,1024,128]{2,1,0:T(8,128)(2,1)S(1)} %get-tuple-element.52), channel_id=1, source_target_pairs={{0,2},{2,0},{4,6},{6,4},{8,10},{10,8},{12,14},{14,12},{16,18},{18,... | collective-permute-start | bytes 1572872 | tf_op jit(solution)/shard_map/ppermute | solution.py:203
  81.6 22.1 %collective-permute-start.12 = (bf16[2,1024,128]{2,1,0:T(8,128)(2,1)S(1)}, bf16[2,1024,128]{2,1,0:T(8,128)(2,1)S(1)}, u32[]{:S(2)}, u32[]{:S(2)}) collective-permute-start(bf16[2,1024,128]{2,1,0:T(8,128)(2,1)S(1)} %fusion.6), channel_id=1, source_target_pairs={{4,0},{6,2},{8,4},{10,6},{12,8},{14,10},{16,12},{18,14},{20,16},{2... | collective-permute-start | bytes 1572872 | tf_op jit(solution)/shard_map/ppermute | solution.py:194
  98.0 21.2 %collective-permute-start.10 = (bf16[2,512,256]{2,1,0:T(8,128)(2,1)}, bf16[2,512,256]{2,1,0:T(8,128)(2,1)S(1)}, u32[]{:S(2)}, u32[]{:S(2)}) collective-permute-start(bf16[2,512,256]{2,1,0:T(8,128)(2,1)} %get-tuple-element.84), channel_id=1, source_target_pairs={{0,1},{1,0},{2,3},{3,2},{4,5},{5,4},{6,7},{7,6},{8,9},{9,8},{10,11... | collective-permute-start | bytes 1572872 | tf_op jit(solution)/shard_map/ppermute | solution.py:199
  99.1 5.5 %collective-permute-start.11 = (bf16[2,1024,128]{2,1,0:T(8,128)(2,1)S(1)}, bf16[2,1024,128]{2,1,0:T(8,128)(2,1)S(1)}, u32[]{:S(2)}, u32[]{:S(2)}) collective-permute-start(bf16[2,1024,128]{2,1,0:T(8,128)(2,1)S(1)} %get-tuple-element.62), channel_id=1, source_target_pairs={{0,2},{2,0},{4,6},{6,4},{8,10},{10,8},{12,14},{14,12},{16,18},{18,... | collective-permute-start | bytes 1572872 | tf_op jit(solution)/shard_map/ppermute | solution.py:203
  104.8 12.1 %collective-permute-start.13 = (bf16[2,512,128]{2,1,0:T(8,128)(2,1)S(1)}, bf16[2,512,128]{2,1,0:T(8,128)(2,1)}, u32[]{:S(2)}, u32[]{:S(2)}) collective-permute-start(bf16[2,512,128]{2,1,0:T(8,128)(2,1)S(1)} %get-tuple-element.82), channel_id=1, source_target_pairs={{4,0},{6,2},{8,4},{10,6},{12,8},{14,10},{16,12},{18,14},{20,16},{2... | collective-permute-start | bytes 786440 | tf_op jit(solution)/shard_map/ppermute | solution.py:194
  106.7 12.8 %collective-permute-start.14 = (bf16[2,512,128]{2,1,0:T(8,128)(2,1)}, bf16[2,512,128]{2,1,0:T(8,128)(2,1)S(1)}, u32[]{:S(2)}, u32[]{:S(2)}) collective-permute-start(bf16[2,512,128]{2,1,0:T(8,128)(2,1)} %get-tuple-element.85), channel_id=1, source_target_pairs={{0,1},{1,0},{2,3},{3,2},{4,5},{5,4},{6,7},{7,6},{8,9},{9,8},{10,11... | collective-permute-start | bytes 786440 | tf_op jit(solution)/shard_map/ppermute | solution.py:199
  107.9 12.8 %collective-permute-start.16 = (bf16[2,512,128]{2,1,0:T(8,128)(2,1)S(1)}, bf16[2,512,128]{2,1,0:T(8,128)(2,1)S(1)}, u32[]{:S(2)}, u32[]{:S(2)}) collective-permute-start(bf16[2,512,128]{2,1,0:T(8,128)(2,1)S(1)} %get-tuple-element.81), channel_id=1, source_target_pairs={{4,0},{6,2},{8,4},{10,6},{12,8},{14,10},{16,12},{18,14},{20,16},{2... | collective-permute-start | bytes 786440 | tf_op jit(solution)/shard_map/ppermute | solution.py:194
  118.0 6.4 %collective-permute-start.15 = (bf16[2,512,128]{2,1,0:T(8,128)(2,1)S(1)}, bf16[2,512,128]{2,1,0:T(8,128)(2,1)S(1)}, u32[]{:S(2)}, u32[]{:S(2)}) collective-permute-start(bf16[2,512,128]{2,1,0:T(8,128)(2,1)S(1)} %fusion.12), channel_id=1, source_target_pairs={{0,1},{1,0},{2,3},{3,2},{4,5},{5,4},{6,7},{7,6},{8,9},{9,8},{10,11... | collective-permute-start | bytes 786440 | tf_op jit(solution)/shard_map/ppermute | solution.py:199
  124.7 1.3 %copy-start.2 = (bf16[2,512,1024]{2,1,0:T(8,128)(2,1)}, bf16[2,512,1024]{2,1,0:T(8,128)(2,1)S(1)}, u32[]{:S(2)}) copy-start(bf16[2,512,1024]{2,1,0:T(8,128)(2,1)S(1)} %fusion.20) | copy-start | bytes 6291460
